TPU v7x, 512 devices: a whole 4x8x8 slice. The times are simulated.
512 devices in a mesh: shot: 64 (over y_hi, x, z), dom: 8 (over y_lo, core).
Axes of the slice: x: 4, y: 8 (y_hi: 2, y_lo: 4; y = y_hi * 4 + y_lo), z: 8, core: 2. Of those that a mesh axis runs over, the one named last changes fastest.
Arguments:
- kappa: float32 [128, 128, 128], P('dom'), may hold values from 0.08 to 0.18
- source_pair: bfloat16 [64, 2, 128, 128, 128], P('shot', None, 'dom'), may hold values from -6 to 6
- adjoint_pair: bfloat16 [64, 2, 128, 128, 128], P('shot', None, 'dom'), may hold values from -6 to 6
- wavelet: float32 [64, 4], P('shot'), may hold values from -6 to 6
- residuals: float32 [64, 4, 256], P('shot'), may hold values from -6 to 6
- source_cell: int32 [64, 3], P('shot'), may hold values from 0 to 127, as said below
- receiver_cells: int32 [64, 3, 256], P('shot'), may hold values from 0 to 127, as said below
Outputs:
- direction: float32 [128, 128, 128], P('dom', 'shot')
Inputs may be any that keep to these rules, and one draw needn't show every extreme that they name: `source_cell`: each shot's source cell as depth, first lateral and second lateral index, below 128, 128 and 128 in turn; the first shot's source lies in the cell (0, 0, 0) and the last shot's in the cell (127, 127, 127). `receiver_cells`: each receiver's cell as depth, first lateral and second lateral index (dimension 1), below 128, 128 and 128 in turn; receivers may coincide; in every shot one receiver lies in the cell (0, 0, 0) and one in the cell (127, 127, 127).
All inputs are finite; a program needn't handle non-finite values.
Results may differ from a plain program's by a relative error of at most 0.0004.
Values sent between devices are 32-bit elements; how exact they have to be, the bound alone decides.
A program may use at most 192 MiB of HBM per device.

v0:
```python
import jax
import jax.numpy as jnp
from jax import lax
from jax.sharding import PartitionSpec as P

STEPS = 2
SEGS = 2


COEFFS = (-205.0 / 72.0, 8.0 / 5.0, -1.0 / 5.0, 8.0 / 315.0, -1.0 / 560.0)
BINOMIAL = (0.0625, 0.25, 0.375, 0.25, 0.0625)


def extended(block, sides, width):
    for axis, dim in sides:
        count = lax.axis_size(axis)
        forward = [(i, i + 1) for i in range(count - 1)]
        backward = [(target, source) for source, target in forward]
        low = lax.ppermute(
            lax.slice_in_dim(block, block.shape[dim] - width, None, axis=dim), axis, forward
        )
        high = lax.ppermute(lax.slice_in_dim(block, 0, width, axis=dim), axis, backward)
        block = jnp.concatenate([low, block, high], axis=dim)
    return block


def stencil(padded, fields):
    depth = fields.shape[1]
    width = fields.shape[2]
    span = fields.shape[3]
    lateral = jnp.pad(fields, ((0, 0), (0, 0), (4, 4), (4, 4)))
    summed = 3.0 * COEFFS[0] * fields
    for shift in range(1, 5):
        summed = summed + COEFFS[shift] * (
            padded[:, 4 + shift : 4 + shift + depth]
            + padded[:, 4 - shift : 4 - shift + depth]
            + lateral[:, :, 4 + shift : 4 + shift + width, 4 : 4 + span]
            + lateral[:, :, 4 - shift : 4 - shift + width, 4 : 4 + span]
            + lateral[:, :, 4 : 4 + width, 4 + shift : 4 + shift + span]
            + lateral[:, :, 4 : 4 + width, 4 - shift : 4 - shift + span]
        )
    return summed


def laplace_pair(fields):
    padded = extended(fields, (("dom", 1),), 4)
    return stencil(padded, fields)


def injectors(depth_line, width, span, cell, receivers):
    first_line = lax.iota(jnp.int32, width)
    second_line = lax.iota(jnp.int32, span)
    source_spot = (
        (depth_line == cell[0]).astype(jnp.float32)[:, None, None]
        * (first_line == cell[1]).astype(jnp.float32)[None, :, None]
        * (second_line == cell[2]).astype(jnp.float32)[None, None, :]
    )
    receiver_plane = (depth_line[:, None] == receivers[0][None, :]).astype(jnp.float32)[
        :, None, :
    ] * (first_line[:, None] == receivers[1][None, :]).astype(jnp.float32)[None, :, :]
    receiver_plane = receiver_plane.reshape(depth_line.shape[0] * width, -1)
    receiver_second = (receivers[2][:, None] == second_line[None, :]).astype(jnp.float32)
    return (source_spot, receiver_plane, receiver_second)


def blur_padded(padded, count, axis):
    summed = jnp.zeros_like(lax.slice_in_dim(padded, 0, count, axis=axis))
    for offset in range(5):
        summed = summed + BINOMIAL[offset] * lax.slice_in_dim(
            padded, offset, offset + count, axis=axis
        )
    return summed


def blur_second(field):
    padded = jnp.pad(field, ((0, 0), (0, 0), (2, 2)))
    return blur_padded(padded, field.shape[2], 2)


def per_device(kappa, source_pair, adjoint_pair, wavelet, residuals, source_cell, receiver_cells):
    depth, width, span = kappa.shape
    anchor = lax.axis_index("dom") * depth
    current = jnp.stack((source_pair[0, 0], adjoint_pair[0, 0])).astype(jnp.float32)
    later = jnp.stack((source_pair[0, 1], adjoint_pair[0, 1])).astype(jnp.float32)
    cell = source_cell[0]
    receivers = receiver_cells[0]
    parts = []
    depth_line = lax.iota(jnp.int32, depth) + anchor
    source_spot, receiver_plane, receiver_second = injectors(
        depth_line, width, span, cell, receivers
    )
    kappa_both = kappa[None]
    for segment in reversed(range(SEGS)):
        gradient = jnp.zeros(kappa.shape, jnp.float32)
        for moment in reversed(range(segment * STEPS, (segment + 1) * STEPS)):
            curvature = kappa_both * laplace_pair(current)
            source_term = wavelet[0, moment] * source_spot
            receiver_term = jnp.dot(
                receiver_plane * residuals[0, moment][None, :],
                receiver_second,
                precision=lax.Precision.HIGHEST,
            ).reshape(depth, width, span)
            inject = jnp.stack((source_term, receiver_term))
            earlier = 2.0 * current - later + curvature + inject
            gradient = gradient + current[1] * (curvature[0] + source_term)
            later, current = (current, earlier)
        parts.append(gradient)
    summed = lax.psum_scatter(parts[0] + parts[1], "shot", scatter_dimension=1, tiled=True)
    rimmed = extended(summed, (("shot", 1),), 2)
    smoothed = blur_second(blur_padded(rimmed, summed.shape[1], 1))
    power = lax.psum(jnp.sum(smoothed * smoothed), ("shot", "dom"))
    cells = depth * lax.axis_size("dom") * width * span
    return -smoothed * lax.rsqrt(power / cells + 1e-06)


def solution(mesh):
    return jax.shard_map(
        per_device,
        mesh=mesh,
        in_specs=(
            P("dom", None, None),
            P("shot", None, "dom", None, None),
            P("shot", None, "dom", None, None),
            P("shot", None),
            P("shot", None, None),
            P("shot", None),
            P("shot", None, None),
        ),
        out_specs=P("dom", "shot", None),
        check_vma=False,
    )
```

profile of v0, /device:TPU:1, one launch (start us, length us, event | category | flops | bytes accessed | tf_op | source)
XLA Modules:
  0.0 681.1 jit_solution(4387165948654795818)
XLA Ops:
  6.5 2.7 slice_bitcast_fusion.9
  9.2 0.0 copy-start.14
  9.3 0.0 copy-start.17
  9.3 0.0 copy-start.16
  9.3 0.1 fusion.182
  9.4 1.3 fusion.190
  10.7 8.8 %collective-permute-start = (f32[2,4,128,128]{3,2,1,0:T(8,128)}, f32[2,4,128,128]{3,2,1,0:T(8,128)}, u32[]{:S(2)}, u32[]{:S(2)}) collective-permute-start(f32[2,4,128,128]{3,2,1,0:T(8,128)} %get-tuple-element.29), channel_id=1, source_target_pairs={{1,0},{2,1},{3,2},{4,3},{5,4},{6,5},{7,6},{9,8},{10,9},{11,10},{12... | collective-permute-start | bytes 1572872 | tf_op jit(solution)/shard_map/ppermute | solution.py:22
  19.5 1.9 collective-permute-start.1
  21.5 0.0 copy-done.15
  21.5 0.6 fusion.194
  22.1 0.6 compare_convert_fusion.3
  22.7 0.6 compare_convert_fusion.1
  23.4 0.6 compare_convert_fusion.2
  24.0 0.7 fusion.193
  24.8 0.1 compare_convert_fusion
  24.9 1.2 fusion.130
  26.1 0.1 broadcast_multiply_fusion
  26.2 2.4 multiply_multiply_fusion.11
  28.6 0.0 collective-permute-done
  28.6 0.0 collective-permute-done.1
  28.6 0.0 copy-done.2
  28.6 0.0 copy-done.3
  28.6 0.0 copy-done.6
  28.6 0.0 copy-done.8
  28.6 0.0 copy-done.11
  28.7 0.0 copy-done.12
  28.7 8.1 %maximum_add_fusion = (f32[2,16,128,128]{3,2,1,0:T(8,128)S(1)}, f32[2,16,128,128]{3,2,1,0:T(8,128)}) fusion(f32[1,16,128,128]{3,2,1,0:T(8,128)S(1)} %fusion.130, f32[1,16,128,128]{3,2,1,0:T(8,128)S(1)} %get-tuple-element.37, bf16[1,16,128,128]{3,2,1,0:T(8,128)(2,1)S(1)} %copy-done.11, bf16[1,16,128,128]{3,2,1,0:T(8,128)(2,1)S(1)} %copy-done.12, ...), kind=kLoop, calls=%fused_computation.255 | loop fusion | flops 24641536 | bytes 12582912 | tf_op jit(solution)/shard_map/add | solution.py:104
  36.7 0.1 fusion.189
  36.8 3.2 collective-permute-start.2
  40.0 2.4 collective-permute-start.3
  42.4 1.2 fusion.129
  43.7 3.7 collective-permute-done.2
  47.3 1.2 collective-permute-done.3
  48.5 7.4 %maximum_add_fusion.1 = (f32[2,16,128,128]{3,2,1,0:T(8,128)S(1)}, f32[2,16,128,128]{3,2,1,0:T(8,128)S(1)}) fusion(f32[1,16,128,128]{3,2,1,0:T(8,128)S(1)} %fusion.129, f32[1,16,128,128]{3,2,1,0:T(8,128)S(1)} %get-tuple-element.35, f32[2,16,128,128]{3,2,1,0:T(8,128)S(1)} %get-tuple-element.11, bf16[1,16,128,128]{3,2,1,0:T(8,128)(2,1)S(1)} %copy-done.6, ...), kind=kLoop, calls=%fused_computation.256 | loop fusion | flops 23592960 | bytes 11534336 | tf_op jit(solution)/shard_map/add | solution.py:104
  55.9 0.0 copy-start.1
  55.9 0.0 copy-start.4
  55.9 0.1 fusion.188
  56.0 1.9 collective-permute-start.4
  57.9 4.4 collective-permute-start.5
  62.3 2.2 fusion.128
  64.5 2.7 collective-permute-done.4
  67.3 1.2 collective-permute-done.5
  68.4 0.8 copy-done.13
  69.2 10.2 %maximum_add_fusion.2 = (f32[2,16,128,128]{3,2,1,0:T(8,128)S(1)}, f32[2,16,128,128]{3,2,1,0:T(8,128)}) fusion(f32[1,16,128,128]{3,2,1,0:T(8,128)} %fusion.128, f32[1,16,128,128]{3,2,1,0:T(8,128)S(1)} %get-tuple-element.36, f32[2,16,128,128]{3,2,1,0:T(8,128)S(1)} %get-tuple-element.11, f32[1,16,128,128]{3,2,1,0:T(8,128)S(1)} %fusion.129, ...), kind=kLoop, calls=%fused_computation.257 | loop fusion | flops 26214400 | bytes 17825792 | tf_op jit(solution)/shard_map/add | solution.py:104
  79.4 0.1 fusion.187
  79.5 1.9 collective-permute-start.6
  81.4 4.6 collective-permute-start.7
  86.0 4.7 collective-permute-done.6
  90.8 1.2 collective-permute-done.7
  92.0 0.8 copy-done.10
  92.8 3.3 fusion.3
  96.1 8.5 %fusion.9 = (f32[2,16,128,128]{3,2,1,0:T(8,128)}, f32[2,16,128,128]{3,2,1,0:T(8,128)}, f32[2,16,128,128]{3,2,1,0:T(8,128)}, f32[2,16,128,128]{3,2,1,0:T(8,128)},...) fusion(f32[2,16,128,128]{3,2,1,0:T(8,128)S(1)} %get-tuple-element.7, ...), kind=kLoop, calls=%fused_computation.128 | loop fusion | flops 8912896 | bytes 17825792 | tf_op jit(solution)/shard_map/add | solution.py:35
  104.6 9.5 %fusion.134 = f32[16,128,128]{2,1,0:T(8,128)S(1)} fusion(f32[2,16,128,128]{3,2,1,0:T(8,128)} %get-tuple-element.18, f32[2,16,128,128]{3,2,1,0:T(8,128)} %get-tuple-element.17, f32[2,16,128,128]{3,2,1,0:T(8,128)} %get-tuple-element.22, f32[2,16,128,128]{3,2,1,0:T(8,128)} %get-tuple-element.16, f32[2,16,128,128]{3,2,1,0:T(8,128)} %get-tuple-element.14, ...), kind=kLoop, calls=%fused_computation.268 | loop fusion | flops 8388608 | bytes 20980240 | tf_op jit(solution)/shard_map/add | solution.py:108
  114.2 1.6 copy.8
  115.7 0.0 reduce-scatter.2.cloned.1.call-update
  115.8 394.4 %reduce-scatter.2.cloned.1.call-done = f32[16,2,128]{2,0,1:T(8,128)} async-done(((f32[16,128,128]{2,0,1:T(8,128)}), f32[16,2,128]{2,0,1:T(8,128)}) %reduce-scatter.2.cloned.1.call-update) | async-done | bytes 16400 | tf_op jit(solution)/shard_map/reduce_scatter | solution.py:108
  510.2 1.3 collective-permute-start.9
  511.5 4.0 collective-permute-start.8
  515.5 0.0 collective-permute-done.9
  515.5 1.1 collective-permute-done.8
  516.6 0.8 fusion.178
  517.3 0.7 multiply_reduce_fusion
  518.0 154.9 %psum.7 = f32[]{:T(128)} all-reduce(f32[]{:T(128)} %get-tuple-element.5), channel_id=1, replica_groups=mesh['shot'=64,'dom'=8] {'shot','dom'}, use_global_device_ids=true, to_apply=%region_2.3 | all-reduce | flops 1 | bytes 8 | tf_op jit(solution)/shard_map/psum | solution.py:111
  673.7 0.6 copy.9
  (28 shorter events, 0.1 us)
Async XLA Ops:
  6.5 503.7 %reduce-scatter.2.cloned.1.call-start = ((), (), s32[]{:S(2)}) async-start(), calls=%async_computation.1 | async-start | bytes 1064960 | tf_op jit(solution)/shard_map/reduce_scatter | solution.py:108
  9.2 1.5 copy-start.5
  9.2 1.5 copy-start.7
  9.2 12.2 %copy-start.15 = (s32[1,3]{1,0:T(1,128)S(1)}, s32[1,3]{1,0:T(1,128)}, u32[]{:S(2)}) copy-start(s32[1,3]{1,0:T(1,128)} %param.12) | copy-start | bytes 40
  9.2 14.8 %copy-start.14 = (f32[1,4]{1,0:T(1,128)S(1)}, f32[1,4]{1,0:T(1,128)}, u32[]{:S(2)}) copy-start(f32[1,4]{1,0:T(1,128)} %param.10) | copy-start | bytes 52
  9.3 15.5 %copy-start.17 = (f32[1,4,256]{2,1,0:T(4,128)S(1)}, f32[1,4,256]{2,1,0:T(4,128)}, u32[]{:S(2)}) copy-start(f32[1,4,256]{2,1,0:T(4,128)} %param.11) | copy-start | bytes 12292
  9.3 15.5 %copy-start.16 = (s32[1,3,256]{2,0,1:T(1,128)S(1)}, s32[1,3,256]{2,0,1:T(1,128)}, u32[]{:S(2)}) copy-start(s32[1,3,256]{2,0,1:T(1,128)} %param.13) | copy-start | bytes 9220
  9.4 19.2 %copy-start.2 = (f32[2,16,128,128]{3,2,1,0:T(8,128)}, f32[2,16,128,128]{3,2,1,0:T(8,128)S(1)}, u32[]{:S(2)}) copy-start(f32[2,16,128,128]{3,2,1,0:T(8,128)S(1)} %fusion.182) | copy-start | bytes 6291460
  10.7 17.8 %collective-permute-start = (f32[2,4,128,128]{3,2,1,0:T(8,128)}, f32[2,4,128,128]{3,2,1,0:T(8,128)}, u32[]{:S(2)}, u32[]{:S(2)}) collective-permute-start(f32[2,4,128,128]{3,2,1,0:T(8,128)} %get-tuple-element.29), channel_id=1, source_target_pairs={{1,0},{2,1},{3,2},{4,3},{5,4},{6,5},{7,6},{9,8},{10,9},{11,10},{12... | collective-permute-start | bytes 1572872 | tf_op jit(solution)/shard_map/ppermute | solution.py:22
  19.5 9.1 %collective-permute-start.1 = (f32[2,4,128,128]{3,2,1,0:T(8,128)}, f32[2,4,128,128]{3,2,1,0:T(8,128)}, u32[]{:S(2)}, u32[]{:S(2)}) collective-permute-start(f32[2,4,128,128]{3,2,1,0:T(8,128)} %get-tuple-element.30), channel_id=1, source_target_pairs={{0,1},{1,2},{2,3},{3,4},{4,5},{5,6},{6,7},{8,9},{9,10},{10,11},{11... | collective-permute-start | bytes 1572872 | tf_op jit(solution)/shard_map/ppermute | solution.py:19
  24.8 3.8 copy-start.3
  24.8 3.8 copy-start.6
  24.8 3.8 copy-start.8
  24.8 3.8 copy-start.11
  24.9 3.8 copy-start.12
  36.7 32.5 %copy-start = (f32[2,16,128,128]{3,2,1,0:T(8,128)}, f32[2,16,128,128]{3,2,1,0:T(8,128)S(1)}, u32[]{:S(2)}) copy-start(f32[2,16,128,128]{3,2,1,0:T(8,128)S(1)} %get-tuple-element.11) | copy-start | bytes 6291460
  36.8 10.5 %collective-permute-start.2 = (f32[2,4,128,128]{3,2,1,0:T(8,128)S(1)}, f32[2,4,128,128]{3,2,1,0:T(8,128)S(1)}, u32[]{:S(2)}, u32[]{:S(2)}) collective-permute-start(f32[2,4,128,128]{3,2,1,0:T(8,128)S(1)} %get-tuple-element.27), channel_id=1, source_target_pairs={{1,0},{2,1},{3,2},{4,3},{5,4},{6,5},{7,6},{9,8},{10,9},{11,10},{12... | collective-permute-start | bytes 1572872 | tf_op jit(solution)/shard_map/ppermute | solution.py:22
  40.0 8.5 %collective-permute-start.3 = (f32[2,4,128,128]{3,2,1,0:T(8,128)S(1)}, f32[2,4,128,128]{3,2,1,0:T(8,128)S(1)}, u32[]{:S(2)}, u32[]{:S(2)}) collective-permute-start(f32[2,4,128,128]{3,2,1,0:T(8,128)S(1)} %get-tuple-element.28), channel_id=1, source_target_pairs={{0,1},{1,2},{2,3},{3,4},{4,5},{5,6},{6,7},{8,9},{9,10},{10,11},{11... | collective-permute-start | bytes 1572872 | tf_op jit(solution)/shard_map/ppermute | solution.py:19
  55.9 23.5 %copy-start.1 = (f32[2,16,128,128]{3,2,1,0:T(8,128)}, f32[2,16,128,128]{3,2,1,0:T(8,128)S(1)}, u32[]{:S(2)}) copy-start(f32[2,16,128,128]{3,2,1,0:T(8,128)S(1)} %get-tuple-element.9) | copy-start | bytes 6291460
  55.9 23.5 %copy-start.4 = (f32[2,16,128,128]{3,2,1,0:T(8,128)}, f32[2,16,128,128]{3,2,1,0:T(8,128)S(1)}, u32[]{:S(2)}) copy-start(f32[2,16,128,128]{3,2,1,0:T(8,128)S(1)} %get-tuple-element.10) | copy-start | bytes 6291460
  56.0 11.2 %collective-permute-start.4 = (f32[2,4,128,128]{3,2,1,0:T(8,128)S(1)}, f32[2,4,128,128]{3,2,1,0:T(8,128)S(1)}, u32[]{:S(2)}, u32[]{:S(2)}) collective-permute-start(f32[2,4,128,128]{3,2,1,0:T(8,128)S(1)} %get-tuple-element.25), channel_id=1, source_target_pairs={{1,0},{2,1},{3,2},{4,3},{5,4},{6,5},{7,6},{9,8},{10,9},{11,10},{12... | collective-permute-start | bytes 1572872 | tf_op jit(solution)/shard_map/ppermute | solution.py:22
  57.9 10.5 %collective-permute-start.5 = (f32[2,4,128,128]{3,2,1,0:T(8,128)S(1)}, f32[2,4,128,128]{3,2,1,0:T(8,128)S(1)}, u32[]{:S(2)}, u32[]{:S(2)}) collective-permute-start(f32[2,4,128,128]{3,2,1,0:T(8,128)S(1)} %get-tuple-element.26), channel_id=1, source_target_pairs={{0,1},{1,2},{2,3},{3,4},{4,5},{5,6},{6,7},{8,9},{9,10},{10,11},{11... | collective-permute-start | bytes 1572872 | tf_op jit(solution)/shard_map/ppermute | solution.py:19
  68.4 0.8 copy-start.13
  79.5 11.2 %collective-permute-start.6 = (f32[2,4,128,128]{3,2,1,0:T(8,128)S(1)}, f32[2,4,128,128]{3,2,1,0:T(8,128)S(1)}, u32[]{:S(2)}, u32[]{:S(2)}) collective-permute-start(f32[2,4,128,128]{3,2,1,0:T(8,128)S(1)} %get-tuple-element.23), channel_id=1, source_target_pairs={{1,0},{2,1},{3,2},{4,3},{5,4},{6,5},{7,6},{9,8},{10,9},{11,10},{12... | collective-permute-start | bytes 1572872 | tf_op jit(solution)/shard_map/ppermute | solution.py:22
  81.4 10.5 %collective-permute-start.7 = (f32[2,4,128,128]{3,2,1,0:T(8,128)S(1)}, f32[2,4,128,128]{3,2,1,0:T(8,128)S(1)}, u32[]{:S(2)}, u32[]{:S(2)}) collective-permute-start(f32[2,4,128,128]{3,2,1,0:T(8,128)S(1)} %get-tuple-element.24), channel_id=1, source_target_pairs={{0,1},{1,2},{2,3},{3,4},{4,5},{5,6},{6,7},{8,9},{9,10},{10,11},{11... | collective-permute-start | bytes 1572872 | tf_op jit(solution)/shard_map/ppermute | solution.py:19
  90.8 1.2 copy-start.9
  91.9 0.8 copy-start.10
  510.2 5.3 collective-permute-start.9
  511.5 5.1 collective-permute-start.8
Sparse Core Ops, SparseCore 0:
  115.9 394.2 reduce-scatter.1
where the time goes:
time: 682 us; the launch traced here: 681 us
  waiting for transfers between devices  410 us (60%)
  blocking collectives  155 us (23%)
  other arithmetic  53.1 us (8%)
  starting transfers between devices  34.3 us (5%)
  between operations  14.5 us (2%)
  local copies, waits for them, and re-layouts  9.37 us (1%)
    reduce_scatter x1, waiting for transfers between devices, per_device(): lax.psum_scatter(parts[0] + parts[1], 'shot', scatter_dimension=1, tiled=...  394 us
    psum x1, blocking collectives, per_device(): power = lax.psum(jnp.sum(smoothed * smoothed), ('shot', 'dom'))  155 us
    add x3, other arithmetic, per_device(): earlier = 2.0 * current - later + curvature + inject  25.7 us
    ppermute x5, starting transfers between devices, extended(): lax.ppermute(lax.slice_in_dim(block, block.shape[dim] - width, None, axis...  17.2 us
    ppermute x5, starting transfers between devices, extended(): lax.ppermute(lax.slice_in_dim(block, 0, width, axis=dim), axis, backward)  17.1 us
  transfers between devices with their start and end apart: 11, of which 8 were waited for; matrix products, arithmetic and copies ran while one was open for 2% of the time, Pallas kernels for 0%

commit v1 on v0

v1 whole, which is shorter than its diff:
```python
import functools

import jax
import jax.numpy as jnp
from jax import lax
from jax.experimental import pallas as pl
from jax.experimental.pallas import tpu as pltpu
from jax.sharding import PartitionSpec as P

MESH = pl.DeviceIdType.MESH
LEVELS = 4
HALO = 4
SCALE = 5040.0
RING = (8064.0, -1008.0, 128.0, -9.0)
CENTER = 3.0 * -14350.0
SHOT_PARTS = (2, 4, 8)
CHUNKS = 2
F32 = jnp.float32
BF16 = jnp.bfloat16


def split(value):
    high = value.astype(BF16)
    low = (value - high.astype(F32)).astype(BF16)
    return high, low


def band(size, weights):
    rows = lax.broadcasted_iota(jnp.int32, (size, size), 0)
    columns = lax.broadcasted_iota(jnp.int32, (size, size), 1)
    distance = jnp.abs(rows - columns)
    matrix = jnp.zeros((size, size), F32)
    for d, weight in enumerate(weights):
        matrix = jnp.where(distance == d, weight, matrix)
    return matrix


def dot(a, b):
    return jnp.dot(a, b, preferred_element_type=F32)


def wave_kernel(
    doms, kappa_hbm, source_hbm, adjoint_hbm, wave, residual, cell, receiver, out,
    kappa, given, field, total, spot, marks, row_side, column_side, blur_row, blur_column,
    load_sem, send_sem, recv_sem,
):
    depth, width, span = kappa.shape
    shot, dom = lax.axis_index("shot"), lax.axis_index("dom")
    core = dom % 2
    anchor = dom * depth

    loads = []
    for at, (source, target) in enumerate(
        (
            (source_hbm.at[0], given.at[0, 0]),
            (adjoint_hbm.at[0], given.at[1, 0]),
            (kappa_hbm, kappa),
            (source_hbm.at[1], given.at[0, 1]),
            (adjoint_hbm.at[1], given.at[1, 1]),
        )
    ):
        copy = pltpu.make_async_copy(source, target, load_sem.at[at])
        copy.start()
        loads.append(copy)

    barrier = pltpu.get_barrier_semaphore()

    @pl.when(dom > 0)
    def _():
        pl.semaphore_signal(barrier, inc=1, device_id=(shot, dom - 1), device_id_type=MESH)

    @pl.when(dom < doms - 1)
    def _():
        pl.semaphore_signal(barrier, inc=1, device_id=(shot, dom + 1), device_id_type=MESH)

    @pl.when(dom == 0)
    def _():
        field[:, :, 0:HALO] = jnp.zeros((2, LEVELS, HALO, width, span), F32)

    @pl.when(dom == doms - 1)
    def _():
        field[:, :, HALO + depth :] = jnp.zeros((2, LEVELS, HALO, width, span), F32)

    def beside(side):
        neighbour = dom + 2 * side - 1
        return neighbour, (neighbour >= 0) & (neighbour < doms)

    def halo_copy(which, level, side):
        neighbour, _ = beside(side)
        return pltpu.make_async_remote_copy(
            src_ref=field.at[which, level, pl.ds(HALO + (depth - HALO) * side, HALO)],
            dst_ref=field.at[which, level, pl.ds((HALO + depth) * (1 - side), HALO)],
            send_sem=send_sem.at[which, level, side],
            recv_sem=recv_sem.at[which, level, 1 - side],
            device_id=(shot, neighbour),
            device_id_type=MESH,
        )

    def halo_send(which, level, side):
        @pl.when(beside(side)[1])
        def _():
            halo_copy(which, level, side).start()

    def halo_wait(which, level, side):
        @pl.when(beside(side)[1])
        def _():
            pltpu.make_async_remote_copy(
                src_ref=field.at[which, level, pl.ds(HALO + (depth - HALO) * side, HALO)],
                dst_ref=field.at[which, level, pl.ds((HALO + depth) * side, HALO)],
                send_sem=send_sem.at[which, level, side],
                recv_sem=recv_sem.at[which, level, side],
                device_id=(shot, beside(side)[0]),
                device_id_type=MESH,
            ).wait_recv()

    neighbours = jnp.where(dom > 0, 1, 0) + jnp.where(dom < doms - 1, 1, 0)
    for which in (0, 1):
        loads[which].wait()
        for side in (0, 1):
            start = (depth - HALO) * side
            field[which, LEVELS - 1, start + HALO : start + 2 * HALO] = given[
                which, 0, start : start + HALO
            ].astype(F32)
        if which == 0:
            pl.semaphore_wait(barrier, neighbours)
        for turn in (0, 1):
            halo_send(which, LEVELS - 1, turn ^ core)
    for which in (0, 1):

        @pl.loop(HALO, depth - HALO)
        def _(z):
            field[which, LEVELS - 1, z + HALO] = given[which, 0, z].astype(F32)

    taps = band(width, (0.0,) + RING).astype(BF16)
    row_side[...] = jnp.concatenate((taps, taps), axis=1)
    taps = band(span, (0.0,) + RING).astype(BF16)
    lines = lax.broadcasted_iota(jnp.int32, (span, receiver.shape[1]), 0)
    for level in range(1, LEVELS):
        spread = jnp.where(lines == receiver[2:3, :], residual[level : level + 1, :], 0.0)
        high, low = split(jnp.transpose(spread))
        column_side[level] = jnp.concatenate((taps, taps, high, low), axis=0)
    first = lax.broadcasted_iota(jnp.int32, (width, span), 0) == cell[1]
    second = lax.broadcasted_iota(jnp.int32, (width, span), 1) == cell[2]
    spot[...] = jnp.where(first & second, 1.0, 0.0)
    lines = lax.broadcasted_iota(jnp.int32, (width, receiver.shape[1]), 0)

    @pl.loop(0, depth)
    def _(z):
        hit = (lines == receiver[1:2, :]) & (receiver[0:1, :] == anchor + z)
        marks[z] = jnp.where(hit, 1.0, 0.0).astype(BF16)

    parts_y, parts_x, parts_z = SHOT_PARTS
    rows = width // (parts_y * parts_x * parts_z)
    place = lax.broadcasted_iota(jnp.int32, (width, width), 0)
    row = place % rows
    y_hi = place // rows % parts_y
    z_at = place // (rows * parts_y) % parts_z
    x_at = place // (rows * parts_y * parts_z)
    wanted = ((y_hi * parts_x + x_at) * parts_z + z_at) * rows + row
    distance = jnp.abs(wanted - lax.broadcasted_iota(jnp.int32, (width, width), 1))
    taps = jnp.zeros((width, width), F32)
    for d, weight in enumerate((6.0, 4.0, 1.0)):
        taps = jnp.where(distance == d, weight / 16.0, taps)
    taps = taps.astype(BF16)
    blur_row[...] = jnp.concatenate((taps, taps), axis=1)
    taps = band(span, (0.375, 0.25, 0.0625)).astype(BF16)
    blur_column[...] = jnp.concatenate((taps, taps), axis=0)

    def advance(which, level, z):
        current = field[which, level, z + HALO]
        if level == LEVELS - 1:
            high = given[which, 0, z]
            upright, flat, skip = high, [high], span
            left = row_side[:, :width]
        else:
            high, low = split(current)
            upright, flat, skip = jnp.concatenate((high, low), axis=0), [high, low], 0
            left = row_side[...]
        if which == 1:
            flat = flat + [marks[z], marks[z]]
            right = column_side[level, skip:]
        else:
            right = column_side[1, skip : 2 * span]
        if len(flat) > 1:
            flat = jnp.concatenate(flat, axis=1)
        else:
            flat = flat[0]
        if which == 1:
            cut = 2 * span - skip
            lateral = dot(left, upright) + dot(flat[:, :cut], right[:cut])
            inject = dot(flat[:, cut:], right[cut:])
        else:
            lateral = dot(left, upright) + dot(flat, right)
            inject = jnp.where(cell[0] == anchor + z, wave[level], 0.0) * spot[...]
        summed = lateral + CENTER * current
        for shift in range(1, HALO + 1):
            summed = summed + RING[shift - 1] * (
                field[which, level, z + HALO + shift] + field[which, level, z + HALO - shift]
            )
        term = kappa[z] * (summed * (1.0 / SCALE)) + inject
        if which == 0:
            part = field[1, level, z + HALO] * term
            if level < LEVELS - 1:
                part = part + total[z]
            if level > 0:
                total[z] = part
            else:
                high, low = split(part)
                part = dot(jnp.concatenate((high, low), axis=1), blur_column[...])
                high, low = split(part)
                out[z] = dot(blur_row[...], jnp.concatenate((high, low), axis=0))
        if level > 0:
            if level == LEVELS - 1:
                later = given[which, 1, z].astype(F32)
            else:
                later = field[which, level + 1, z + HALO]
            field[which, level - 1, z + HALO] = 2.0 * current - later + term

    def run(which, level, start, count):
        @pl.loop(0, count)
        def _(i):
            advance(which, level, start + i)

    for load in loads[2:]:
        load.wait()
    for level in reversed(range(LEVELS)):
        fields = (0, 1) if level > 0 else (0,)
        if level == LEVELS - 1:
            for which in fields:
                run(which, level, HALO, depth - 2 * HALO)
        for turn in (0, 1):
            side = turn ^ core
            for which in fields:
                halo_wait(which, level, side)
                run(which, level, (depth - HALO) * side, HALO)
                if level > 1 or (level == 1 and which == 0):
                    halo_send(which, level - 1, side)
        if level < LEVELS - 1:
            for which in fields:
                run(which, level, HALO, depth - 2 * HALO)

    for level in reversed(range(LEVELS)):
        for which in (0, 1) if level > 0 else (0,):
            for side in (0, 1):

                @pl.when(beside(side)[1])
                def _():
                    halo_copy(which, level, side).wait_send()


def sum_kernel(
    doms, cells, part, out,
    x_in, z_out, z_in, y_out, y_in, power_out, power_in,
    x_send, x_recv, z_send, z_recv, y_send, y_recv, p_send, p_recv,
):
    depth, width, span = part.shape
    shot, dom = lax.axis_index("shot"), lax.axis_index("dom")
    parts_y, parts_x, parts_z = SHOT_PARTS
    rows = width // (parts_y * parts_x * parts_z)
    z_at, x_at, y_at = shot % parts_z, shot // parts_z % parts_x, shot // (parts_z * parts_x)
    layers = depth // CHUNKS
    stripe = width // parts_x

    def by_x(step):
        return ((y_at * parts_x + (x_at + step) % parts_x) * parts_z + z_at, dom)

    def by_z(step):
        return ((y_at * parts_x + x_at) * parts_z + (z_at + step) % parts_z, dom)

    def by_xy(step):
        at = (y_at * parts_x + x_at + step) % (parts_x * parts_y)
        return (at * parts_z + z_at, dom)

    def by_dom(step):
        return (shot, (dom + step) % doms)

    barrier = pltpu.get_barrier_semaphore()
    peers = [by_dom(step) for step in range(1, doms)]
    peers += [by_z(step) for step in range(1, parts_z)]
    peers += [by_xy(step) for step in range(1, parts_x * parts_y)]
    for peer in peers:
        pl.semaphore_signal(barrier, inc=1, device_id=peer, device_id_type=MESH)
    pl.semaphore_wait(barrier, len(peers))

    def send(source, target, send_sem, recv_sem, peer):
        copy = pltpu.make_async_remote_copy(
            src_ref=source,
            dst_ref=target,
            send_sem=send_sem,
            recv_sem=recv_sem,
            device_id=peer,
            device_id_type=MESH,
        )
        copy.start()
        return copy

    sent = []
    x_copies = [[] for _ in range(CHUNKS)]
    for chunk in range(CHUNKS):
        for step in range(1, parts_x):
            start = pl.multiple_of((x_at + step) % parts_x * stripe, stripe)
            x_copies[chunk].append(
                send(
                    part.at[pl.ds(chunk * layers, layers), pl.ds(start, stripe)],
                    x_in.at[chunk, step - 1],
                    x_send.at[chunk, step - 1],
                    x_recv.at[chunk, step - 1],
                    by_x(step),
                )
            )
    count = layers * stripe
    to = lax.broadcasted_iota(jnp.int32, (count, count), 0)
    row = to % rows
    layer = to // rows % layers
    y_hi = to // (rows * layers) % parts_y
    z_of = to // (rows * layers * parts_y)
    wanted = ((layer * parts_z + z_of) * parts_y + y_hi) * rows + row
    order = wanted == lax.broadcasted_iota(jnp.int32, (count, count), 1)
    order = jnp.where(order, 1.0, 0.0).astype(BF16)
    own = pl.multiple_of(x_at * stripe, stripe)
    z_copies = [[] for _ in range(CHUNKS)]
    for chunk in range(CHUNKS):
        summed = part[pl.ds(chunk * layers, layers), pl.ds(own, stripe)]
        for step in range(1, parts_x):
            x_copies[chunk][step - 1].wait_recv()
            summed = summed + x_in[chunk, step - 1]
        high, low = split(summed.reshape(count, span))
        moved = dot(order, high) + dot(order, low)
        z_out[chunk] = moved.reshape(parts_z, count // parts_z, span)
        for step in range(1, parts_z):
            z_copies[chunk].append(
                send(
                    z_out.at[chunk, (z_at + step) % parts_z],
                    z_in.at[chunk, step - 1],
                    z_send.at[chunk, step - 1],
                    z_recv.at[chunk, step - 1],
                    by_z(step),
                )
            )
    block = rows * layers
    for chunk in range(CHUNKS):
        summed = z_out[chunk, z_at]
        for step in range(1, parts_z):
            z_copies[chunk][step - 1].wait_recv()
            summed = summed + z_in[chunk, step - 1]
        for y_hi in range(parts_y):
            y_out[y_hi, chunk * block : (chunk + 1) * block] = summed[
                y_hi * block : (y_hi + 1) * block
            ]
    summed = y_out[y_at]
    y_copies = []
    for step in range(1, parts_y):
        y_copies.append(
            send(
                y_out.at[(y_at + step) % parts_y],
                y_in.at[step - 1],
                y_send.at[step - 1],
                y_recv.at[step - 1],
                by_xy(step * parts_x),
            )
        )
    for step in range(1, parts_y):
        y_copies[step - 1].wait_recv()
        summed = summed + y_in[step - 1]
    squares = summed * summed
    power = squares[0:8]
    for at in range(8, rows * depth, 8):
        power = power + squares[at : at + 8]
    p_copies = []
    for stage, (size, by) in enumerate(
        ((doms, by_dom), (parts_z, by_z), (parts_x * parts_y, by_xy))
    ):
        power_out[stage] = power
        now = [
            send(
                power_out.at[stage],
                power_in.at[stage, step - 1],
                p_send.at[stage, step - 1],
                p_recv.at[stage, step - 1],
                by(step),
            )
            for step in range(1, size)
        ]
        for step in range(1, size):
            now[step - 1].wait_recv()
            power = power + power_in[stage, step - 1]
        p_copies += now
    power = jnp.sum(power)
    out[...] = -summed * lax.rsqrt(jnp.full((1, 1), power) * (1.0 / cells) + 1e-6)
    for copies in x_copies + z_copies + [y_copies, p_copies]:
        for copy in copies:
            copy.wait_send()


def per_device(doms, kappa, source_pair, adjoint_pair, wavelet, residuals, source_cell, receiver_cells):
    depth, width, span = kappa.shape
    receivers = receiver_cells.shape[2]
    parts_y, parts_x, parts_z = SHOT_PARTS
    layers = depth // CHUNKS
    rows = width // (parts_y * parts_x * parts_z)
    plane = (width, span)
    hbm = pl.BlockSpec(memory_space=pl.ANY)
    vmem = pl.BlockSpec(memory_space=pltpu.VMEM)
    smem = pl.BlockSpec(memory_space=pltpu.SMEM)
    dma = pltpu.SemaphoreType.DMA
    part = pl.pallas_call(
        functools.partial(wave_kernel, doms),
        out_shape=jax.ShapeDtypeStruct(kappa.shape, F32),
        in_specs=[hbm, hbm, hbm, smem, vmem, smem, vmem],
        out_specs=vmem,
        scratch_shapes=[
            pltpu.VMEM(kappa.shape, F32),
            pltpu.VMEM((2, 2, depth) + plane, BF16),
            pltpu.VMEM((2, LEVELS, depth + 2 * HALO) + plane, F32),
            pltpu.VMEM(kappa.shape, F32),
            pltpu.VMEM(plane, F32),
            pltpu.VMEM((depth, width, receivers), BF16),
            pltpu.VMEM((width, 2 * width), BF16),
            pltpu.VMEM((LEVELS, 2 * span + 2 * receivers, span), BF16),
            pltpu.VMEM((width, 2 * width), BF16),
            pltpu.VMEM((2 * span, span), BF16),
            dma((5,)),
            dma((2, LEVELS, 2)),
            dma((2, LEVELS, 2)),
        ],
        compiler_params=pltpu.CompilerParams(
            collective_id=0, has_side_effects=True, vmem_limit_bytes=40 * 2**20
        ),
    )(
        kappa,
        source_pair[0],
        adjoint_pair[0],
        wavelet[0],
        residuals[0],
        source_cell[0],
        receiver_cells[0],
    )
    stages = 3
    most = max(doms, parts_z, parts_x * parts_y) - 1
    stripe = width // parts_x
    piece = layers * stripe // parts_z
    direction = pl.pallas_call(
        functools.partial(sum_kernel, doms, float(depth * doms * width * span)),
        out_shape=jax.ShapeDtypeStruct((depth * rows, span), F32),
        in_specs=[vmem],
        out_specs=vmem,
        scratch_shapes=[
            pltpu.VMEM((CHUNKS, parts_x - 1, layers, stripe, span), F32),
            pltpu.VMEM((CHUNKS, parts_z, piece, span), F32),
            pltpu.VMEM((CHUNKS, parts_z - 1, piece, span), F32),
            pltpu.VMEM((parts_y, depth * rows, span), F32),
            pltpu.VMEM((parts_y - 1, depth * rows, span), F32),
            pltpu.VMEM((stages, 8, span), F32),
            pltpu.VMEM((stages, most, 8, span), F32),
            dma((CHUNKS, parts_x - 1)),
            dma((CHUNKS, parts_x - 1)),
            dma((CHUNKS, parts_z - 1)),
            dma((CHUNKS, parts_z - 1)),
            dma((parts_y - 1,)),
            dma((parts_y - 1,)),
            dma((stages, most)),
            dma((stages, most)),
        ],
        compiler_params=pltpu.CompilerParams(
            collective_id=1, has_side_effects=True, vmem_limit_bytes=40 * 2**20
        ),
    )(part)
    return direction.reshape(depth, rows, span)


def solution(mesh):
    return jax.shard_map(
        functools.partial(per_device, mesh.shape["dom"]),
        mesh=mesh,
        in_specs=(
            P("dom", None, None),
            P("shot", None, "dom", None, None),
            P("shot", None, "dom", None, None),
            P("shot", None),
            P("shot", None, None),
            P("shot", None),
            P("shot", None, None),
        ),
        out_specs=P("dom", "shot", None),
        check_vma=False,
    )
```

time: 682 us -> 95.5 us (0.14)
  waiting for transfers between devices: 410 us -> 0 us
  blocking collectives: 155 us -> 0 us
  Pallas kernels: 0 us -> 89.5 us
  other arithmetic: 53.1 us -> 0 us
  starting transfers between devices: 34.3 us -> 0 us
  between operations: 14.5 us -> 0.03 us
    reduce_scatter x1 -> x0, waiting for transfers between devices: 394 us -> none  [per_device(): lax.psum_scatter(parts[0] + parts[1], 'shot', scatter_dimension=1, tiled=...]
    psum x1 -> x0, blocking collectives: 155 us -> none  [per_device(): power = lax.psum(jnp.sum(smoothed * smoothed), ('shot', 'dom'))]
    pallas_call x0 -> x2, Pallas kernels: none -> 89.5 us  [the longest x1 46.9 us: per_device(): pl.pallas_call(functools.partial(sum_kernel, doms, float(depth * doms * w...]
    add x8 -> x0, other arithmetic: 47.8 us -> none  [the longest x3 25.7 us: per_device(): earlier = 2.0 * current - later + curvature + inject]
    ppermute x10 -> x0, starting transfers between devices: 34.3 us -> none  [the longest x5 17.2 us: extended(): lax.ppermute(lax.slice_in_dim(block, block.shape[dim] - width, None, axis...]
    ppermute x10 -> x0, waiting for transfers between devices: 15.7 us -> none  [the longest x5 11.1 us: extended(): lax.ppermute(lax.slice_in_dim(block, 0, width, axis=dim), axis, backward)]
  transfers between devices with their start and end apart: 11 -> 0, of which waited for: 8 -> 0; matrix products, arithmetic and copies ran while one was open for 2% -> 0% of each run, Pallas kernels for 0% -> 0%
where the time goes in v1:
time: 95.5 us; the launch traced here: 95.2 us
  Pallas kernels  89.5 us (94%)
  local copies, waits for them, and re-layouts  5.65 us (6%)
    pallas_call x1, Pallas kernels, per_device(): pl.pallas_call(functools.partial(sum_kernel, doms, float(depth * doms * w...  46.9 us
    pallas_call x1, Pallas kernels, per_device(): pl.pallas_call(functools.partial(wave_kernel, doms), out_shape=jax.ShapeD...  42.6 us
    unnamed x16, local copies, waits for them, and re-layouts  5.65 us

profile of v1, /device:TPU:1, one launch (start us, length us, event | category | flops | bytes accessed | tf_op | source)
XLA Modules:
  0.0 95.2 jit_solution(13915230054096411321)
XLA Ops:
  0.0 0.0 copy-start.6
  0.0 0.7 copy-done.6
  0.7 0.0 copy-start.3
  0.7 0.0 copy-start.4
  0.7 0.0 copy-start.5
  0.7 0.7 copy-done.3
  1.4 0.0 copy-done.4
  1.4 0.0 copy-done.5
  1.4 0.0 copy-start
  1.4 1.2 %copy-done = f32[16,128,128]{2,1,0:T(8,128)S(1)} copy-done((f32[16,128,128]{2,1,0:T(8,128)S(1)}, f32[16,128,128]{2,1,0:T(8,128)}, u32[]{:S(2)}) %copy-start) | copy-done | bytes 1048600
  2.6 0.0 copy-start.1
  2.6 1.2 %copy-done.1 = bf16[1,2,16,128,128]{4,3,2,1,0:T(8,128)(2,1)S(1)} copy-done((bf16[1,2,16,128,128]{4,3,2,1,0:T(8,128)(2,1)S(1)}, bf16[1,2,16,128,128]{4,3,2,1,0:T(8,128)(2,1)}, u32[]{:S(2)}) %copy-start.1) | copy-done | bytes 1048600
  3.8 0.0 copy-start.2
  3.8 1.2 %copy-done.2 = bf16[1,2,16,128,128]{4,3,2,1,0:T(8,128)(2,1)S(1)} copy-done((bf16[1,2,16,128,128]{4,3,2,1,0:T(8,128)(2,1)S(1)}, bf16[1,2,16,128,128]{4,3,2,1,0:T(8,128)(2,1)}, u32[]{:S(2)}) %copy-start.2) | copy-done | bytes 1048600
  5.1 42.6 %shard_map.73.part = f32[16,128,128]{2,1,0:T(8,128)S(1)} custom-call(f32[16,128,128]{2,1,0:T(8,128)S(1)} %copy-done, bf16[2,16,128,128]{3,2,1,0:T(8,128)(2,1)S(1)} %bitcast.9, bf16[2,16,128,128]{3,2,1,0:T(8,128)(2,1)S(1)} %bitcast.10, f32[4]{0:T(128)S(1)} %bitcast.14, f32[4,256]{1,0:T(4,128)S(1)} %bitcast.13, s32[3]{0:T(128)S(1)} %bitcast.15, ...), custom_call_target="tpu_custom_call" | custom-call | tf_op jit(solution)/shard_map/pallas_call | solution.py:406
  47.7 46.9 %shard_map.74 = f32[32,128]{1,0:T(8,128)S(1)} custom-call(f32[16,128,128]{2,1,0:T(8,128)S(1)} %shard_map.73.part), custom_call_target="tpu_custom_call" | custom-call | tf_op jit(solution)/shard_map/pallas_call | solution.py:442
  94.6 0.6 copy.12
  (1 shorter events, 0.0 us)
Async XLA Ops:
  0.0 0.7 copy-start.6
  0.7 0.7 copy-start.3
  0.7 0.7 copy-start.4
  0.7 0.7 copy-start.5
  1.4 1.2 %copy-start = (f32[16,128,128]{2,1,0:T(8,128)S(1)}, f32[16,128,128]{2,1,0:T(8,128)}, u32[]{:S(2)}) copy-start(f32[16,128,128]{2,1,0:T(8,128)} %kappa_hbm.1) | copy-start | bytes 3145732
  2.6 1.2 %copy-start.1 = (bf16[1,2,16,128,128]{4,3,2,1,0:T(8,128)(2,1)S(1)}, bf16[1,2,16,128,128]{4,3,2,1,0:T(8,128)(2,1)}, u32[]{:S(2)}) copy-start(bf16[1,2,16,128,128]{4,3,2,1,0:T(8,128)(2,1)} %param.8) | copy-start | bytes 3145732
  3.8 1.2 %copy-start.2 = (bf16[1,2,16,128,128]{4,3,2,1,0:T(8,128)(2,1)S(1)}, bf16[1,2,16,128,128]{4,3,2,1,0:T(8,128)(2,1)}, u32[]{:S(2)}) copy-start(bf16[1,2,16,128,128]{4,3,2,1,0:T(8,128)(2,1)} %param.9) | copy-start | bytes 3145732

commit v2 on v0

v2 whole, which is shorter than its diff:
```python
import functools

import jax
import jax.numpy as jnp
from jax import lax
from jax.experimental import pallas as pl
from jax.experimental.pallas import tpu as pltpu
from jax.sharding import PartitionSpec as P

MESH = pl.DeviceIdType.MESH
LEVELS = 4
HALO = 4
SCALE = 5040.0
RING = (8064.0, -1008.0, 128.0, -9.0)
CENTER = 3.0 * -14350.0
SHOT_PARTS = (2, 4, 8)
F32 = jnp.float32
BF16 = jnp.bfloat16


def split(value):
    high = value.astype(BF16)
    low = (value - high.astype(F32)).astype(BF16)
    return high, low


def band(size, weights):
    rows = lax.broadcasted_iota(jnp.int32, (size, size), 0)
    columns = lax.broadcasted_iota(jnp.int32, (size, size), 1)
    distance = jnp.abs(rows - columns)
    matrix = jnp.zeros((size, size), F32)
    for d, weight in enumerate(weights):
        matrix = jnp.where(distance == d, weight, matrix)
    return matrix


def twice(matrix, axis):
    matrix = matrix.astype(BF16)
    return jnp.concatenate((matrix, matrix), axis=axis)


def dot(a, b):
    return jnp.dot(a, b, preferred_element_type=F32)


def rows_of(blocks):
    return jnp.concatenate(blocks, axis=0)


def columns_of(blocks):
    return jnp.concatenate(blocks, axis=1)


def kernel(
    doms, cells,
    kappa_hbm, source_hbm, adjoint_hbm, wave, residual, cell, receiver, out,
    kappa, given, fields, totals, part, spot, marks, row_side, column_side, inject_side,
    blur_row, blur_column, order,
    x_in, z_out, z_in, y_out, y_in, power_out, power_in,
    load_sem, halo_send, halo_recv,
    x_send, x_recv, z_send, z_recv, y_send, y_recv, p_send, p_recv,
):
    depth, width, span = kappa.shape
    chunks = depth // HALO
    shot, dom = lax.axis_index("shot"), lax.axis_index("dom")
    core = dom % 2
    anchor = dom * depth
    parts_y, parts_x, parts_z = SHOT_PARTS
    rows = width // (parts_y * parts_x * parts_z)
    z_at, x_at, y_at = shot % parts_z, shot // parts_z % parts_x, shot // (parts_z * parts_x)
    stripe = width // parts_x

    def by_x(step):
        return ((y_at * parts_x + (x_at + step) % parts_x) * parts_z + z_at, dom)

    def by_z(step):
        return ((y_at * parts_x + x_at) * parts_z + (z_at + step) % parts_z, dom)

    def by_y(step):
        at = (y_at * doms + dom + step) % (parts_y * doms)
        return ((at // doms * parts_x + x_at) * parts_z + z_at, at % doms)

    loads = []
    for at, (source, target) in enumerate(
        (
            (source_hbm.at[0], given[0][0]),
            (adjoint_hbm.at[0], given[1][0]),
            (kappa_hbm, kappa),
            (source_hbm.at[1], given[0][1]),
            (adjoint_hbm.at[1], given[1][1]),
        )
    ):
        copy = pltpu.make_async_copy(source, target, load_sem.at[at])
        copy.start()
        loads.append(copy)

    barrier = pltpu.get_barrier_semaphore()
    stages = (
        [by_y(step) for step in range(1, parts_y * doms)],
        [by_z(step) for step in range(1, parts_z)],
        [by_x(step) for step in range(1, parts_x)],
    )
    peers = [peer for stage in stages for peer in stage]
    for peer in peers:
        pl.semaphore_signal(barrier, inc=1, device_id=peer, device_id_type=MESH)

    @pl.when(dom == 0)
    def _():
        for which in (0, 1):
            for level in range(LEVELS):
                fields[which][level][0:HALO] = jnp.zeros((HALO, width, span), F32)

    @pl.when(dom == doms - 1)
    def _():
        for which in (0, 1):
            for level in range(LEVELS):
                fields[which][level][HALO + depth :] = jnp.zeros((HALO, width, span), F32)

    def beside(side):
        neighbour = dom + 2 * side - 1
        return neighbour, (neighbour >= 0) & (neighbour < doms)

    def halo_copy(which, level, side, landing):
        field = fields[which][level]
        return pltpu.make_async_remote_copy(
            src_ref=field.at[pl.ds(HALO + (depth - HALO) * side, HALO)],
            dst_ref=field.at[pl.ds((HALO + depth) * landing, HALO)],
            send_sem=halo_send.at[which, level, side],
            recv_sem=halo_recv.at[which, level, landing],
            device_id=(shot, beside(side)[0]),
            device_id_type=MESH,
        )

    def halo_start(which, level, side):
        @pl.when(beside(side)[1])
        def _():
            halo_copy(which, level, side, 1 - side).start()

    def halo_wait(which, level, side):
        @pl.when(beside(side)[1])
        def _():
            halo_copy(which, level, side, side).wait_recv()

    for which in (0, 1):
        loads[which].wait()
        field = fields[which][LEVELS - 1]
        for start in (0, depth - HALO):
            field[start + HALO : start + 2 * HALO] = given[which][0][
                start : start + HALO
            ].astype(F32)
        if which == 0:
            pl.semaphore_wait(barrier, len(peers))
        for turn in (0, 1):
            halo_start(which, LEVELS - 1, turn ^ core)
    for which in (0, 1):
        fields[which][LEVELS - 1][2 * HALO : depth] = given[which][0][
            HALO : depth - HALO
        ].astype(F32)

    row_side[...] = twice(band(width, (0.0,) + RING), 1)
    column_side[...] = twice(band(span, (0.0,) + RING), 0)
    first = lax.broadcasted_iota(jnp.int32, (width, span), 0) == cell[1]
    second = lax.broadcasted_iota(jnp.int32, (width, span), 1) == cell[2]
    spot[...] = jnp.where(first & second, 1.0, 0.0)
    lines = lax.broadcasted_iota(jnp.int32, (span, receiver.shape[2]), 0)
    for level in range(1, LEVELS):
        spread = jnp.where(lines == receiver[2], residual[level : level + 1, :], 0.0)
        inject_side[level] = columns_of(split(jnp.transpose(spread)))
    lines = lax.broadcasted_iota(jnp.int32, (width, receiver.shape[2]), 0)

    @pl.loop(0, depth)
    def _(z):
        hit = (lines == receiver[1]) & (receiver[0] == anchor + z)
        marks[z] = jnp.where(hit, 1.0, 0.0).astype(BF16)

    place = lax.broadcasted_iota(jnp.int32, (width, width), 0)
    row = place % rows
    y_hi = place // rows % parts_y
    z_of = place // (rows * parts_y) % parts_z
    x_of = place // (rows * parts_y * parts_z)
    wanted = ((y_hi * parts_x + x_of) * parts_z + z_of) * rows + row
    distance = jnp.abs(wanted - lax.broadcasted_iota(jnp.int32, (width, width), 1))
    taps = jnp.zeros((width, width), F32)
    for d, weight in enumerate((0.375, 0.25, 0.0625)):
        taps = jnp.where(distance == d, weight, taps)
    blur_row[...] = twice(taps, 1)
    blur_column[...] = twice(band(span, (0.375, 0.25, 0.0625)), 0)
    count = HALO * stripe
    place = lax.broadcasted_iota(jnp.int32, (count, count), 0)
    row = place % rows
    layer = place // rows % HALO
    y_hi = place // (rows * HALO) % parts_y
    z_of = place // (rows * HALO * parts_y)
    wanted = ((layer * parts_z + z_of) * parts_y + y_hi) * rows + row
    hit = wanted == lax.broadcasted_iota(jnp.int32, (count, count), 1)
    order[...] = twice(jnp.where(hit, 1.0, 0.0), 1)

    def both_sides(blocks, left, right):
        flat = rows_of([columns_of(block) for block in blocks])
        upright = columns_of([rows_of(block) for block in blocks])
        flat, upright = dot(flat, right), dot(left, upright)
        return [
            flat[at * width : (at + 1) * width] + upright[:, at * span : (at + 1) * span]
            for at in range(len(blocks))
        ]

    def advance(which, level, start):
        field = fields[which][level]
        layers = range(HALO)
        if level == LEVELS - 1:
            blocks = [(given[which][0][start + at],) for at in layers]
            lateral = both_sides(blocks, row_side[:, :width], column_side[:span])
        else:
            blocks = [split(field[start + at + HALO]) for at in layers]
            lateral = both_sides(blocks, row_side[...], column_side[...])
        if which == 1:
            inject = dot(rows_of([marks[start + at] for at in layers]), inject_side[level])
            inject = inject[:, :span] + inject[:, span:]
            inject = [inject[at * width : (at + 1) * width] for at in layers]
        else:
            inject = [
                jnp.where(cell[0] == anchor + start + at, wave[level], 0.0) * spot[...]
                for at in layers
            ]
        blurred = []
        for at in layers:
            z = start + at
            current = field[z + HALO]
            summed = lateral[at] + CENTER * current
            for shift in range(1, HALO + 1):
                summed = summed + RING[shift - 1] * (
                    field[z + HALO + shift] + field[z + HALO - shift]
                )
            term = kappa[z] * (summed * (1.0 / SCALE)) + inject[at]
            if which == 0:
                product = fields[1][level][z + HALO] * term
                if level < LEVELS - 1:
                    product = product + totals[level][z]
                if level > 0:
                    totals[level - 1][z] = product
                else:
                    blurred.append(product)
            if level > 0:
                if level == LEVELS - 1:
                    later = given[which][1][z].astype(F32)
                else:
                    later = fields[which][level + 1][z + HALO]
                fields[which][level - 1][z + HALO] = 2.0 * current - later + term
        return blurred

    def blur(blurred, start):
        flat = dot(rows_of([columns_of(split(at)) for at in blurred]), blur_column[...])
        blocks = [flat[at * width : (at + 1) * width] for at in range(HALO)]
        upright = dot(blur_row[...], columns_of([rows_of(split(at)) for at in blocks]))
        for at in range(HALO):
            part[start + at] = upright[:, at * span : (at + 1) * span]

    def send(source, target, send_sem, recv_sem, peer):
        copy = pltpu.make_async_remote_copy(
            src_ref=source,
            dst_ref=target,
            send_sem=send_sem,
            recv_sem=recv_sem,
            device_id=peer,
            device_id_type=MESH,
        )
        copy.start()
        return copy

    for load in loads[2:]:
        load.wait()
    for level in reversed(range(1, LEVELS)):
        if level == LEVELS - 1:
            for which in (0, 1):

                @pl.loop(HALO, depth - HALO, step=HALO)
                def _(start):
                    advance(which, level, start)

        @pl.loop(0, 2)
        def _(turn):
            side = turn ^ core
            for which in (0, 1):
                halo_wait(which, level, side)
                advance(which, level, (depth - HALO) * side)
                if level > 1 or which == 0:
                    halo_start(which, level - 1, side)

        if level < LEVELS - 1:
            for which in (0, 1):

                @pl.loop(HALO, depth - HALO, step=HALO)
                def _(start):
                    advance(which, level, start)

    starts = [HALO * at for at in range(1, chunks - 1)]
    starts += [(depth - HALO) * (1 - core), (depth - HALO) * core]
    x_copies, z_copies, y_copies, p_copies = ([[] for _ in starts] for _ in range(4))
    for chunk, start in enumerate(starts):
        if chunk >= chunks - 2:
            halo_wait(0, 0, (1 - core) if chunk == chunks - 2 else core)
        blur(advance(0, 0, start), start)
        for step in range(1, parts_x):
            place = pl.multiple_of((x_at + step) % parts_x * stripe, stripe)
            x_copies[chunk].append(
                send(
                    part.at[pl.ds(start, HALO), pl.ds(place, stripe)],
                    x_in.at[chunk, step - 1],
                    x_send.at[chunk, step - 1],
                    x_recv.at[chunk, step - 1],
                    by_x(step),
                )
            )
    own = pl.multiple_of(x_at * stripe, stripe)
    for chunk, start in enumerate(starts):
        summed = part[pl.ds(start, HALO), pl.ds(own, stripe)]
        for step in range(1, parts_x):
            x_copies[chunk][step - 1].wait_recv()
            summed = summed + x_in[chunk, step - 1]
        moved = dot(order[...], rows_of(split(summed.reshape(count, span))))
        z_out[chunk] = moved.reshape(parts_z, count // parts_z, span)
        for step in range(1, parts_z):
            z_copies[chunk].append(
                send(
                    z_out.at[chunk, (z_at + step) % parts_z],
                    z_in.at[chunk, step - 1],
                    z_send.at[chunk, step - 1],
                    z_recv.at[chunk, step - 1],
                    by_z(step),
                )
            )
    block = rows * HALO
    for chunk in range(chunks):
        summed = z_out[chunk, z_at]
        for step in range(1, parts_z):
            z_copies[chunk][step - 1].wait_recv()
            summed = summed + z_in[chunk, step - 1]
        y_out[chunk] = summed.reshape(parts_y, block, span)
        for step in range(1, parts_y):
            y_copies[chunk].append(
                send(
                    y_out.at[chunk, (y_at + step) % parts_y],
                    y_in.at[chunk, step - 1],
                    y_send.at[chunk, step - 1],
                    y_recv.at[chunk, step - 1],
                    by_y(step * doms),
                )
            )
    pieces = []
    power = jnp.zeros((block, span), F32)
    for chunk in range(chunks):
        summed = y_out[chunk, y_at]
        for step in range(1, parts_y):
            y_copies[chunk][step - 1].wait_recv()
            summed = summed + y_in[chunk, step - 1]
        pieces.append(summed)
        power = power + summed * summed
    for stage, peers in enumerate(stages):
        power_out[stage] = power
        now = [
            send(
                power_out.at[stage],
                power_in.at[stage, step],
                p_send.at[stage, step],
                p_recv.at[stage, step],
                peer,
            )
            for step, peer in enumerate(peers)
        ]
        for step, copy in enumerate(now):
            copy.wait_recv()
            power = power + power_in[stage, step]
        p_copies[0] += now
    scale = lax.rsqrt(jnp.full((1, 1), jnp.sum(power)) * (1.0 / cells) + 1e-6)
    for start, piece in zip(starts, pieces, strict=True):
        place = start * rows
        if not isinstance(place, int):
            place = pl.multiple_of(place, block)
        out[pl.ds(place, block)] = -piece * scale

    for copies in x_copies + z_copies + y_copies + p_copies:
        for copy in copies:
            copy.wait_send()
    for level in reversed(range(LEVELS)):
        for which in (0, 1) if level > 0 else (0,):
            for side in (0, 1):

                @pl.when(beside(side)[1])
                def _():
                    halo_copy(which, level, side, 1 - side).wait_send()


def per_device(doms, kappa, source_pair, adjoint_pair, wavelet, residuals, source_cell, receiver_cells):
    depth, width, span = kappa.shape
    receivers = receiver_cells.shape[2]
    parts_y, parts_x, parts_z = SHOT_PARTS
    rows = width // (parts_y * parts_x * parts_z)
    chunks = depth // HALO
    stripe = width // parts_x
    piece = HALO * stripe // parts_z
    block = rows * HALO
    most = max(doms * parts_y, parts_z, parts_x) - 1
    hbm = pl.BlockSpec(memory_space=pl.ANY)
    vmem = pl.BlockSpec(memory_space=pltpu.VMEM)
    smem = pl.BlockSpec(memory_space=pltpu.SMEM)
    dma = pltpu.SemaphoreType.DMA
    slab = pltpu.VMEM(kappa.shape, F32)
    padded = pltpu.VMEM((depth + 2 * HALO, width, span), F32)
    first = pltpu.VMEM(kappa.shape, BF16)
    direction = pl.pallas_call(
        functools.partial(kernel, doms, float(depth * doms * width * span)),
        out_shape=jax.ShapeDtypeStruct((depth * rows, span), F32),
        in_specs=[hbm, hbm, hbm, smem, vmem, smem, vmem],
        out_specs=vmem,
        scratch_shapes=[
            slab,
            [[first] * 2] * 2,
            [[padded] * LEVELS] * 2,
            [slab] * (LEVELS - 1),
            slab,
            pltpu.VMEM((width, span), F32),
            pltpu.VMEM((depth, width, receivers), BF16),
            pltpu.VMEM((width, 2 * width), BF16),
            pltpu.VMEM((2 * span, span), BF16),
            pltpu.VMEM((LEVELS, receivers, 2 * span), BF16),
            pltpu.VMEM((width, 2 * width), BF16),
            pltpu.VMEM((2 * span, span), BF16),
            pltpu.VMEM((HALO * stripe, 2 * HALO * stripe), BF16),
            pltpu.VMEM((chunks, parts_x - 1, HALO, stripe, span), F32),
            pltpu.VMEM((chunks, parts_z, piece, span), F32),
            pltpu.VMEM((chunks, parts_z - 1, piece, span), F32),
            pltpu.VMEM((chunks, parts_y, block, span), F32),
            pltpu.VMEM((chunks, parts_y - 1, block, span), F32),
            pltpu.VMEM((3, block, span), F32),
            pltpu.VMEM((3, most, block, span), F32),
            dma((5,)),
            dma((2, LEVELS, 2)),
            dma((2, LEVELS, 2)),
            dma((chunks, parts_x - 1)),
            dma((chunks, parts_x - 1)),
            dma((chunks, parts_z - 1)),
            dma((chunks, parts_z - 1)),
            dma((chunks, parts_y - 1)),
            dma((chunks, parts_y - 1)),
            dma((3, most)),
            dma((3, most)),
        ],
        compiler_params=pltpu.CompilerParams(
            collective_id=0, has_side_effects=True, vmem_limit_bytes=60 * 2**20
        ),
    )(
        kappa,
        source_pair[0],
        adjoint_pair[0],
        wavelet[0],
        residuals[0],
        source_cell[0],
        jnp.transpose(receiver_cells, (1, 0, 2)),
    )
    return direction.reshape(depth, rows, span)


def solution(mesh):
    return jax.shard_map(
        functools.partial(per_device, mesh.shape["dom"]),
        mesh=mesh,
        in_specs=(
            P("dom", None, None),
            P("shot", None, "dom", None, None),
            P("shot", None, "dom", None, None),
            P("shot", None),
            P("shot", None, None),
            P("shot", None),
            P("shot", None, None),
        ),
        out_specs=P("dom", "shot", None),
        check_vma=False,
    )
```

time: 682 us -> 76.8 us (0.11)
  waiting for transfers between devices: 410 us -> 0 us
  blocking collectives: 155 us -> 0 us
  Pallas kernels: 0 us -> 75.1 us
  other arithmetic: 53.1 us -> 0 us
  starting transfers between devices: 34.3 us -> 0 us
  between operations: 14.5 us -> 0.01 us
  local copies, waits for them, and re-layouts: 9.37 us -> 1.32 us
    reduce_scatter x1 -> x0, waiting for transfers between devices: 394 us -> none  [per_device(): lax.psum_scatter(parts[0] + parts[1], 'shot', scatter_dimension=1, tiled=...]
    psum x1 -> x0, blocking collectives: 155 us -> none  [per_device(): power = lax.psum(jnp.sum(smoothed * smoothed), ('shot', 'dom'))]
    pallas_call x0 -> x1, Pallas kernels: none -> 75.1 us  [per_device(): pl.pallas_call(functools.partial(kernel, doms, float(depth * doms * width...]
    add x8 -> x0, other arithmetic: 47.8 us -> none  [the longest x3 25.7 us: per_device(): earlier = 2.0 * current - later + curvature + inject]
    ppermute x10 -> x0, starting transfers between devices: 34.3 us -> none  [the longest x5 17.2 us: extended(): lax.ppermute(lax.slice_in_dim(block, block.shape[dim] - width, None, axis...]
    ppermute x10 -> x0, waiting for transfers between devices: 15.7 us -> none  [the longest x5 11.1 us: extended(): lax.ppermute(lax.slice_in_dim(block, 0, width, axis=dim), axis, backward)]
  transfers between devices with their start and end apart: 11 -> 0, of which waited for: 8 -> 0; matrix products, arithmetic and copies ran while one was open for 2% -> 0% of each run, Pallas kernels for 0% -> 0%
where the time goes in v2:
time: 76.8 us; the launch traced here: 76.4 us
  Pallas kernels  75.1 us (98%)
  local copies, waits for them, and re-layouts  1.32 us (2%)
    pallas_call x1, Pallas kernels, per_device(): pl.pallas_call(functools.partial(kernel, doms, float(depth * doms * width...  75.1 us

profile of v2, /device:TPU:1, one launch (start us, length us, event | category | flops | bytes accessed | tf_op | source)
XLA Modules:
  0.0 76.4 jit_solution(7010713142477516062)
XLA Ops:
  0.0 75.1 %shard_map.73 = f32[32,128]{1,0:T(8,128)} custom-call(f32[16,128,128]{2,1,0:T(8,128)} %kappa_hbm.1, bf16[2,16,128,128]{3,2,1,0:T(8,128)(2,1)} %bitcast.7, bf16[2,16,128,128]{3,2,1,0:T(8,128)(2,1)} %bitcast.8, f32[4]{0:T(128)} %bitcast.12, f32[4,256]{1,0:T(4,128)} %bitcast.10, s32[3]{0:T(128)} %bitcast.13, s32[3,1,256]{2,1,0:T(1,128)} %bitcast.11), custom_call_target="tpu_custom_call" | custom-call | tf_op jit(solution)/shard_map/pallas_call | solution.py:410
  75.1 1.3 %copy.9 = f32[16,2,128]{2,1,0:T(2,128)} copy(f32[16,2,128]{2,1,0:T(2,128)} %bitcast.9) | data formatting | bytes 32768

commit v3 on v2

--- a/solution.py
+++ b/solution.py
@@ -56,19 +56,18 @@
     kappa_hbm, source_hbm, adjoint_hbm, wave, residual, cell, receiver, out,
     kappa, given, fields, totals, part, spot, marks, row_side, column_side, inject_side,
     blur_row, blur_column, order,
-    x_in, z_out, z_in, y_out, y_in, power_out, power_in,
+    first_in, second_out, second_in, y_out, y_in, y_sum, power_out, power_in,
     load_sem, halo_send, halo_recv,
-    x_send, x_recv, z_send, z_recv, y_send, y_recv, p_send, p_recv,
+    first_send, first_recv, second_send, second_recv, y_send, y_recv, p_send, p_recv,
 ):
     depth, width, span = kappa.shape
-    chunks = depth // HALO
     shot, dom = lax.axis_index("shot"), lax.axis_index("dom")
     core = dom % 2
     anchor = dom * depth
     parts_y, parts_x, parts_z = SHOT_PARTS
     rows = width // (parts_y * parts_x * parts_z)
     z_at, x_at, y_at = shot % parts_z, shot // parts_z % parts_x, shot // (parts_z * parts_x)
-    stripe = width // parts_x
+    first_two = ((parts_x, parts_z), (parts_z, parts_x))
 
     def by_x(step):
         return ((y_at * parts_x + (x_at + step) % parts_x) * parts_z + z_at, dom)
@@ -77,8 +76,10 @@
         return ((y_at * parts_x + x_at) * parts_z + (z_at + step) % parts_z, dom)
 
     def by_y(step):
-        at = (y_at * doms + dom + step) % (parts_y * doms)
-        return ((at // doms * parts_x + x_at) * parts_z + z_at, at % doms)
+        return (((y_at + step) % parts_y * parts_x + x_at) * parts_z + z_at, dom)
+
+    def by_dom(step):
+        return (shot, (dom + step) % doms)
 
     loads = []
     for at, (source, target) in enumerate(
@@ -96,11 +97,12 @@
 
     barrier = pltpu.get_barrier_semaphore()
     stages = (
-        [by_y(step) for step in range(1, parts_y * doms)],
+        [by_dom(step) for step in range(1, doms)],
         [by_z(step) for step in range(1, parts_z)],
         [by_x(step) for step in range(1, parts_x)],
     )
     peers = [peer for stage in stages for peer in stage]
+    peers += [by_y(step) for step in range(1, parts_y)]
     for peer in peers:
         pl.semaphore_signal(barrier, inc=1, device_id=peer, device_id_type=MESH)
 
@@ -176,24 +178,27 @@
     place = lax.broadcasted_iota(jnp.int32, (width, width), 0)
     row = place % rows
     y_hi = place // rows % parts_y
-    z_of = place // (rows * parts_y) % parts_z
-    x_of = place // (rows * parts_y * parts_z)
-    wanted = ((y_hi * parts_x + x_of) * parts_z + z_of) * rows + row
-    distance = jnp.abs(wanted - lax.broadcasted_iota(jnp.int32, (width, width), 1))
-    taps = jnp.zeros((width, width), F32)
-    for d, weight in enumerate((0.375, 0.25, 0.0625)):
-        taps = jnp.where(distance == d, weight, taps)
-    blur_row[...] = twice(taps, 1)
+    for way, parts in enumerate(first_two):
+        minor = place // (rows * parts_y) % parts[1]
+        major = place // (rows * parts_y * parts[1])
+        x_of, z_of = (major, minor) if way == 0 else (minor, major)
+        wanted = ((y_hi * parts_x + x_of) * parts_z + z_of) * rows + row
+        distance = jnp.abs(wanted - lax.broadcasted_iota(jnp.int32, (width, width), 1))
+        taps = jnp.zeros((width, width), F32)
+        for d, weight in enumerate((0.375, 0.25, 0.0625)):
+            taps = jnp.where(distance == d, weight, taps)
+        blur_row[way] = twice(taps, 1)
     blur_column[...] = twice(band(span, (0.375, 0.25, 0.0625)), 0)
-    count = HALO * stripe
-    place = lax.broadcasted_iota(jnp.int32, (count, count), 0)
-    row = place % rows
-    layer = place // rows % HALO
-    y_hi = place // (rows * HALO) % parts_y
-    z_of = place // (rows * HALO * parts_y)
-    wanted = ((layer * parts_z + z_of) * parts_y + y_hi) * rows + row
-    hit = wanted == lax.broadcasted_iota(jnp.int32, (count, count), 1)
-    order[...] = twice(jnp.where(hit, 1.0, 0.0), 1)
+    for way, parts in enumerate(first_two):
+        count = HALO * width // parts[0]
+        place = lax.broadcasted_iota(jnp.int32, (count, count), 0)
+        row = place % rows
+        layer = place // rows % HALO
+        y_hi = place // (rows * HALO) % parts_y
+        minor = place // (rows * HALO * parts_y)
+        wanted = ((layer * parts[1] + minor) * parts_y + y_hi) * rows + row
+        hit = wanted == lax.broadcasted_iota(jnp.int32, (count, count), 1)
+        order[way][...] = twice(jnp.where(hit, 1.0, 0.0), 1)
 
     def both_sides(blocks, left, right):
         flat = rows_of([columns_of(block) for block in blocks])
@@ -248,15 +253,15 @@
                 fields[which][level - 1][z + HALO] = 2.0 * current - later + term
         return blurred
 
-    def blur(blurred, start):
+    def blur(blurred, start, way):
         flat = dot(rows_of([columns_of(split(at)) for at in blurred]), blur_column[...])
         blocks = [flat[at * width : (at + 1) * width] for at in range(HALO)]
-        upright = dot(blur_row[...], columns_of([rows_of(split(at)) for at in blocks]))
+        upright = dot(blur_row[way], columns_of([rows_of(split(at)) for at in blocks]))
         for at in range(HALO):
             part[start + at] = upright[:, at * span : (at + 1) * span]
 
-    def send(source, target, send_sem, recv_sem, peer):
-        copy = pltpu.make_async_remote_copy(
+    def remote(source, target, send_sem, recv_sem, peer):
+        return pltpu.make_async_remote_copy(
             src_ref=source,
             dst_ref=target,
             send_sem=send_sem,
@@ -264,101 +269,127 @@
             device_id=peer,
             device_id_type=MESH,
         )
-        copy.start()
-        return copy
-
-    for load in loads[2:]:
-        load.wait()
-    for level in reversed(range(1, LEVELS)):
-        if level == LEVELS - 1:
-            for which in (0, 1):
-
-                @pl.loop(HALO, depth - HALO, step=HALO)
-                def _(start):
-                    advance(which, level, start)
-
+
+    inner, outer = (depth - HALO) * (1 - core), (depth - HALO) * core
+    starts = (HALO, 2 * HALO, inner, outer)
+    ways = (1, 0, 0, 0)
+    spots = (x_at, z_at)
+
+    def first_copy(chunk, step):
+        way = ways[chunk]
+        stripe = width // first_two[way][0]
+        place = (spots[way] + step) % first_two[way][0] * stripe
+        return remote(
+            part.at[pl.ds(starts[chunk], HALO), pl.ds(pl.multiple_of(place, stripe), stripe)],
+            first_in[way].at[max(chunk - 1, 0), step - 1],
+            first_send.at[chunk, step - 1],
+            first_recv.at[chunk, step - 1],
+            (by_x, by_z)[way](step),
+        )
+
+    def second_copy(chunk, step):
+        way = ways[chunk]
+        return remote(
+            second_out[way].at[max(chunk - 1, 0), (spots[1 - way] + step) % first_two[way][1]],
+            second_in[way].at[max(chunk - 1, 0), step - 1],
+            second_send.at[chunk, step - 1],
+            second_recv.at[chunk, step - 1],
+            (by_z, by_x)[way](step),
+        )
+
+    def y_copy(chunk, step):
+        return remote(
+            y_out.at[chunk],
+            y_in.at[chunk, step - 1],
+            y_send.at[chunk, step - 1],
+            y_recv.at[chunk, step - 1],
+            by_y(step),
+        )
+
+    def first_steps(chunk):
+        return range(1, first_two[ways[chunk]][0])
+
+    def second_steps(chunk):
+        return range(1, first_two[ways[chunk]][1])
+
+    def finish(chunk):
+        start = starts[chunk]
+        blur(advance(0, 0, start), start, ways[chunk])
+        for step in first_steps(chunk):
+            first_copy(chunk, step).start()
+
+    def inside(which, level):
+        @pl.loop(HALO, depth - HALO, step=HALO)
+        def _(start):
+            advance(which, level, start)
+
+    def sides(which, level):
         @pl.loop(0, 2)
         def _(turn):
             side = turn ^ core
-            for which in (0, 1):
-                halo_wait(which, level, side)
-                advance(which, level, (depth - HALO) * side)
-                if level > 1 or which == 0:
-                    halo_start(which, level - 1, side)
-
-        if level < LEVELS - 1:
-            for which in (0, 1):
-
-                @pl.loop(HALO, depth - HALO, step=HALO)
-                def _(start):
-                    advance(which, level, start)
-
-    starts = [HALO * at for at in range(1, chunks - 1)]
-    starts += [(depth - HALO) * (1 - core), (depth - HALO) * core]
-    x_copies, z_copies, y_copies, p_copies = ([[] for _ in starts] for _ in range(4))
-    for chunk, start in enumerate(starts):
-        if chunk >= chunks - 2:
-            halo_wait(0, 0, (1 - core) if chunk == chunks - 2 else core)
-        blur(advance(0, 0, start), start)
-        for step in range(1, parts_x):
-            place = pl.multiple_of((x_at + step) % parts_x * stripe, stripe)
-            x_copies[chunk].append(
-                send(
-                    part.at[pl.ds(start, HALO), pl.ds(place, stripe)],
-                    x_in.at[chunk, step - 1],
-                    x_send.at[chunk, step - 1],
-                    x_recv.at[chunk, step - 1],
-                    by_x(step),
-                )
-            )
-    own = pl.multiple_of(x_at * stripe, stripe)
-    for chunk, start in enumerate(starts):
-        summed = part[pl.ds(start, HALO), pl.ds(own, stripe)]
-        for step in range(1, parts_x):
-            x_copies[chunk][step - 1].wait_recv()
-            summed = summed + x_in[chunk, step - 1]
-        moved = dot(order[...], rows_of(split(summed.reshape(count, span))))
-        z_out[chunk] = moved.reshape(parts_z, count // parts_z, span)
-        for step in range(1, parts_z):
-            z_copies[chunk].append(
-                send(
-                    z_out.at[chunk, (z_at + step) % parts_z],
-                    z_in.at[chunk, step - 1],
-                    z_send.at[chunk, step - 1],
-                    z_recv.at[chunk, step - 1],
-                    by_z(step),
-                )
-            )
+            halo_wait(which, level, side)
+            advance(which, level, (depth - HALO) * side)
+            if level > 1 or which == 0:
+                halo_start(which, level - 1, side)
+
+    for load in loads[2:]:
+        load.wait()
+    for which in (0, 1):
+        inside(which, LEVELS - 1)
+    for which in (0, 1):
+        sides(which, LEVELS - 1)
+    for level in reversed(range(2, LEVELS - 1)):
+        for which in (0, 1):
+            sides(which, level)
+            inside(which, level)
+    sides(0, 1)
+    inside(0, 1)
+    inside(1, 1)
+    finish(0)
+    finish(1)
+    for chunk, side in ((2, 1 - core), (3, core)):
+        halo_wait(1, 1, side)
+        advance(1, 1, starts[chunk])
+        halo_wait(0, 0, side)
+        finish(chunk)
+
+    for chunk in (1, 2, 0, 3):
+        way = ways[chunk]
+        parts = first_two[way]
+        stripe = width // parts[0]
+        own = pl.multiple_of(spots[way] * stripe, stripe)
+        summed = part[pl.ds(starts[chunk], HALO), pl.ds(own, stripe)]
+        for step in first_steps(chunk):
+            first_copy(chunk, step).wait_recv()
+            summed = summed + first_in[way][max(chunk - 1, 0), step - 1]
+        moved = dot(order[way][...], rows_of(split(summed.reshape(HALO * stripe, span))))
+        second_out[way][max(chunk - 1, 0)] = moved.reshape(parts[1], HALO * stripe // parts[1], span)
+        for step in second_steps(chunk):
+            second_copy(chunk, step).start()
     block = rows * HALO
-    for chunk in range(chunks):
-        summed = z_out[chunk, z_at]
-        for step in range(1, parts_z):
-            z_copies[chunk][step - 1].wait_recv()
-            summed = summed + z_in[chunk, step - 1]
+    for chunk in (1, 2, 0, 3):
+        way = ways[chunk]
+        summed = second_out[way][max(chunk - 1, 0), spots[1 - way]]
+        for step in second_steps(chunk):
+            second_copy(chunk, step).wait_recv()
+            summed = summed + second_in[way][max(chunk - 1, 0), step - 1]
         y_out[chunk] = summed.reshape(parts_y, block, span)
         for step in range(1, parts_y):
-            y_copies[chunk].append(
-                send(
-                    y_out.at[chunk, (y_at + step) % parts_y],
-                    y_in.at[chunk, step - 1],
-                    y_send.at[chunk, step - 1],
-                    y_recv.at[chunk, step - 1],
-                    by_y(step * doms),
-                )
-            )
-    pieces = []
+            y_copy(chunk, step).start()
     power = jnp.zeros((block, span), F32)
-    for chunk in range(chunks):
-        summed = y_out[chunk, y_at]
+    for chunk in (1, 2, 0, 3):
+        summed = y_out[chunk]
         for step in range(1, parts_y):
-            y_copies[chunk][step - 1].wait_recv()
+            y_copy(chunk, step).wait_recv()
             summed = summed + y_in[chunk, step - 1]
-        pieces.append(summed)
-        power = power + summed * summed
+        y_sum[chunk] = summed
+        for y_hi in range(parts_y):
+            power = power + summed[y_hi] * summed[y_hi]
+    power_copies = []
     for stage, peers in enumerate(stages):
         power_out[stage] = power
         now = [
-            send(
+            remote(
                 power_out.at[stage],
                 power_in.at[stage, step],
                 p_send.at[stage, step],
@@ -367,20 +398,28 @@
             )
             for step, peer in enumerate(peers)
         ]
+        for copy in now:
+            copy.start()
         for step, copy in enumerate(now):
             copy.wait_recv()
             power = power + power_in[stage, step]
-        p_copies[0] += now
+        power_copies += now
     scale = lax.rsqrt(jnp.full((1, 1), jnp.sum(power)) * (1.0 / cells) + 1e-6)
-    for start, piece in zip(starts, pieces, strict=True):
+    for chunk, start in enumerate(starts):
         place = start * rows
         if not isinstance(place, int):
             place = pl.multiple_of(place, block)
-        out[pl.ds(place, block)] = -piece * scale
-
-    for copies in x_copies + z_copies + y_copies + p_copies:
-        for copy in copies:
-            copy.wait_send()
+        out[pl.ds(place, block)] = -y_sum[chunk, y_at] * scale
+
+    for chunk in range(len(starts)):
+        for step in first_steps(chunk):
+            first_copy(chunk, step).wait_send()
+        for step in second_steps(chunk):
+            second_copy(chunk, step).wait_send()
+        for step in range(1, parts_y):
+            y_copy(chunk, step).wait_send()
+    for copy in power_copies:
+        copy.wait_send()
     for level in reversed(range(LEVELS)):
         for which in (0, 1) if level > 0 else (0,):
             for side in (0, 1):
@@ -396,10 +435,9 @@
     parts_y, parts_x, parts_z = SHOT_PARTS
     rows = width // (parts_y * parts_x * parts_z)
     chunks = depth // HALO
-    stripe = width // parts_x
-    piece = HALO * stripe // parts_z
+    counts = (HALO * width // parts_x, HALO * width // parts_z)
     block = rows * HALO
-    most = max(doms * parts_y, parts_z, parts_x) - 1
+    most = max(doms, parts_z, parts_x) - 1
     hbm = pl.BlockSpec(memory_space=pl.ANY)
     vmem = pl.BlockSpec(memory_space=pltpu.VMEM)
     smem = pl.BlockSpec(memory_space=pltpu.SMEM)
@@ -423,30 +461,40 @@
             pltpu.VMEM((width, 2 * width), BF16),
             pltpu.VMEM((2 * span, span), BF16),
             pltpu.VMEM((LEVELS, receivers, 2 * span), BF16),
-            pltpu.VMEM((width, 2 * width), BF16),
+            pltpu.VMEM((2, width, 2 * width), BF16),
             pltpu.VMEM((2 * span, span), BF16),
-            pltpu.VMEM((HALO * stripe, 2 * HALO * stripe), BF16),
-            pltpu.VMEM((chunks, parts_x - 1, HALO, stripe, span), F32),
-            pltpu.VMEM((chunks, parts_z, piece, span), F32),
-            pltpu.VMEM((chunks, parts_z - 1, piece, span), F32),
+            [pltpu.VMEM((count, 2 * count), BF16) for count in counts],
+            [
+                pltpu.VMEM((most, parts - 1, HALO, width // parts, span), F32)
+                for most, parts in ((chunks - 1, parts_x), (1, parts_z))
+            ],
+            [
+                pltpu.VMEM((most, parts, block * parts_y, span), F32)
+                for most, parts in ((chunks - 1, parts_z), (1, parts_x))
+            ],
+            [
+                pltpu.VMEM((most, parts - 1, block * parts_y, span), F32)
+                for most, parts in ((chunks - 1, parts_z), (1, parts_x))
+            ],
             pltpu.VMEM((chunks, parts_y, block, span), F32),
-            pltpu.VMEM((chunks, parts_y - 1, block, span), F32),
+            pltpu.VMEM((chunks, parts_y - 1, parts_y, block, span), F32),
+            pltpu.VMEM((chunks, parts_y, block, span), F32),
             pltpu.VMEM((3, block, span), F32),
             pltpu.VMEM((3, most, block, span), F32),
             dma((5,)),
             dma((2, LEVELS, 2)),
             dma((2, LEVELS, 2)),
-            dma((chunks, parts_x - 1)),
-            dma((chunks, parts_x - 1)),
-            dma((chunks, parts_z - 1)),
-            dma((chunks, parts_z - 1)),
+            dma((chunks, most)),
+            dma((chunks, most)),
+            dma((chunks, most)),
+            dma((chunks, most)),
             dma((chunks, parts_y - 1)),
             dma((chunks, parts_y - 1)),
             dma((3, most)),
             dma((3, most)),
         ],
         compiler_params=pltpu.CompilerParams(
-            collective_id=0, has_side_effects=True, vmem_limit_bytes=60 * 2**20
+            collective_id=0, has_side_effects=True, vmem_limit_bytes=56164352
         ),
     )(
         kappa,

time: 76.8 us -> 69.2 us (0.901)
  Pallas kernels: 75.1 us -> 67.7 us
    pallas_call x1, Pallas kernels: 75.1 us -> 67.7 us  [per_device(): pl.pallas_call(functools.partial(kernel, doms, float(depth * doms * width...]
where the time goes in v3:
time: 69.2 us; the launch traced here: 69 us
  Pallas kernels  67.7 us (98%)
  local copies, waits for them, and re-layouts  1.31 us (2%)
    pallas_call x1, Pallas kernels, per_device(): pl.pallas_call(functools.partial(kernel, doms, float(depth * doms * width...  67.7 us

profile of v3, /device:TPU:1, one launch (start us, length us, event | category | flops | bytes accessed | tf_op | source)
XLA Modules:
  0.0 69.0 jit_solution(3791390847830942212)
XLA Ops:
  0.0 0.0 copy-start.3
  0.0 0.0 copy-start
  0.0 0.0 copy-start.1
  0.0 0.0 copy-start.2
  0.0 0.6 copy-done.3
  0.7 0.0 copy-done
  0.7 0.0 copy-done.1
  0.7 0.0 copy-done.2
  0.7 67.7 %shard_map.73 = f32[32,128]{1,0:T(8,128)S(1)} custom-call(f32[16,128,128]{2,1,0:T(8,128)} %kappa_hbm.1, bf16[2,16,128,128]{3,2,1,0:T(8,128)(2,1)} %bitcast.12, bf16[2,16,128,128]{3,2,1,0:T(8,128)(2,1)} %bitcast.13, f32[4]{0:T(128)S(1)} %bitcast.10, f32[4,256]{1,0:T(4,128)S(1)} %bitcast.8, s32[3]{0:T(128)S(1)} %bitcast.11, s32[3,1,256]{2,1,0:T(1,128)S(1)} %bitcast.9), custom_call_target="tpu_custom_call" | custom-call | tf_op jit(solution)/shard_map/pallas_call | solution.py:448
  68.4 0.6 copy.9
Async XLA Ops:
  0.0 0.7 copy-start.3
  0.0 0.7 %copy-start = (f32[1,4,256]{2,1,0:T(4,128)S(1)}, f32[1,4,256]{2,1,0:T(4,128)}, u32[]{:S(2)}) copy-start(f32[1,4,256]{2,1,0:T(4,128)} %param.11) | copy-start | bytes 12292
  0.0 0.7 %copy-start.1 = (s32[1,3,256]{2,0,1:T(1,128)S(1)}, s32[1,3,256]{2,0,1:T(1,128)}, u32[]{:S(2)}) copy-start(s32[1,3,256]{2,0,1:T(1,128)} %param.13) | copy-start | bytes 9220
  0.0 0.7 %copy-start.2 = (f32[1,4]{1,0:T(1,128)S(1)}, f32[1,4]{1,0:T(1,128)}, u32[]{:S(2)}) copy-start(f32[1,4]{1,0:T(1,128)} %param.10) | copy-start | bytes 52

commit v4 on v3

--- a/solution.py
+++ b/solution.py
@@ -334,19 +334,15 @@
 
     for load in loads[2:]:
         load.wait()
-    for which in (0, 1):
-        inside(which, LEVELS - 1)
-    for which in (0, 1):
-        sides(which, LEVELS - 1)
-    for level in reversed(range(2, LEVELS - 1)):
+    for level in reversed(range(2, LEVELS)):
         for which in (0, 1):
+            inside(which, level)
             sides(which, level)
-            inside(which, level)
-    sides(0, 1)
     inside(0, 1)
     inside(1, 1)
+    sides(0, 1)
+    finish(1)
     finish(0)
-    finish(1)
     for chunk, side in ((2, 1 - core), (3, core)):
         halo_wait(1, 1, side)
         advance(1, 1, starts[chunk])

time: 69.2 us -> 66.6 us (0.962)
  Pallas kernels: 67.7 us -> 65.1 us
    pallas_call x1, Pallas kernels: 67.7 us -> 65.1 us  [per_device(): pl.pallas_call(functools.partial(kernel, doms, float(depth * doms * width...]
where the time goes in v4:
time: 66.6 us; the launch traced here: 66.5 us
  Pallas kernels  65.1 us (98%)
  local copies, waits for them, and re-layouts  1.31 us (2%)
    pallas_call x1, Pallas kernels, per_device(): pl.pallas_call(functools.partial(kernel, doms, float(depth * doms * width...  65.1 us

profile of v4, /device:TPU:1, one launch (start us, length us, event | category | flops | bytes accessed | tf_op | source)
XLA Modules:
  0.0 66.5 jit_solution(16588794807193723029)
XLA Ops:
  0.0 0.0 copy-start.3
  0.0 0.0 copy-start
  0.0 0.0 copy-start.1
  0.0 0.0 copy-start.2
  0.0 0.6 copy-done.3
  0.7 0.0 copy-done
  0.7 0.0 copy-done.1
  0.7 0.0 copy-done.2
  0.7 65.1 %shard_map.73 = f32[32,128]{1,0:T(8,128)S(1)} custom-call(f32[16,128,128]{2,1,0:T(8,128)} %kappa_hbm.1, bf16[2,16,128,128]{3,2,1,0:T(8,128)(2,1)} %bitcast.12, bf16[2,16,128,128]{3,2,1,0:T(8,128)(2,1)} %bitcast.13, f32[4]{0:T(128)S(1)} %bitcast.10, f32[4,256]{1,0:T(4,128)S(1)} %bitcast.8, s32[3]{0:T(128)S(1)} %bitcast.11, s32[3,1,256]{2,1,0:T(1,128)S(1)} %bitcast.9), custom_call_target="tpu_custom_call" | custom-call | tf_op jit(solution)/shard_map/pallas_call | solution.py:444
  65.9 0.6 copy.9
Async XLA Ops:
  0.0 0.7 copy-start.3
  0.0 0.7 %copy-start = (f32[1,4,256]{2,1,0:T(4,128)S(1)}, f32[1,4,256]{2,1,0:T(4,128)}, u32[]{:S(2)}) copy-start(f32[1,4,256]{2,1,0:T(4,128)} %param.11) | copy-start | bytes 12292
  0.0 0.7 %copy-start.1 = (s32[1,3,256]{2,0,1:T(1,128)S(1)}, s32[1,3,256]{2,0,1:T(1,128)}, u32[]{:S(2)}) copy-start(s32[1,3,256]{2,0,1:T(1,128)} %param.13) | copy-start | bytes 9220
  0.0 0.7 %copy-start.2 = (f32[1,4]{1,0:T(1,128)S(1)}, f32[1,4]{1,0:T(1,128)}, u32[]{:S(2)}) copy-start(f32[1,4]{1,0:T(1,128)} %param.10) | copy-start | bytes 52

commit v5 on v4

--- a/solution.py
+++ b/solution.py
@@ -57,7 +57,7 @@
     kappa, given, fields, totals, part, spot, marks, row_side, column_side, inject_side,
     blur_row, blur_column, order,
     first_in, second_out, second_in, y_out, y_in, y_sum, power_out, power_in,
-    load_sem, halo_send, halo_recv,
+    load_sem, known, halo_send, halo_recv,
     first_send, first_recv, second_send, second_recv, y_send, y_recv, p_send, p_recv,
 ):
     depth, width, span = kappa.shape
@@ -68,6 +68,7 @@
     rows = width // (parts_y * parts_x * parts_z)
     z_at, x_at, y_at = shot % parts_z, shot // parts_z % parts_x, shot // (parts_z * parts_x)
     first_two = ((parts_x, parts_z), (parts_z, parts_x))
+    ring = parts_y * doms // 2
 
     def by_x(step):
         return ((y_at * parts_x + (x_at + step) % parts_x) * parts_z + z_at, dom)
@@ -80,6 +81,17 @@
 
     def by_dom(step):
         return (shot, (dom + step) % doms)
+
+    def by_ring(step, turn):
+        at = (y_at * (doms // 2) + dom // 2 + step) % ring
+        y_hi, chip = at // (doms // 2), at % (doms // 2)
+        return ((y_hi * parts_x + x_at) * parts_z + z_at, chip * 2 + (core + turn) % 2)
+
+    def near(size):
+        return sorted({1, size - 1})
+
+    def next_to(size):
+        return [2, size - 2] if size > 4 else []
 
     loads = []
     for at, (source, target) in enumerate(
@@ -101,8 +113,11 @@
         [by_z(step) for step in range(1, parts_z)],
         [by_x(step) for step in range(1, parts_x)],
     )
-    peers = [peer for stage in stages for peer in stage]
-    peers += [by_y(step) for step in range(1, parts_y)]
+    beyond = [by_ring(step, 0) for step in near(ring)]
+    beyond += [by_z(step) for step in near(parts_z)] + [by_x(step) for step in near(parts_x)]
+    peers = [by_ring(2 * core - 1, 1), by_ring(0, 1)] + beyond
+    farther = [by_ring(step, 0) for step in next_to(ring)]
+    farther += [by_z(step) for step in next_to(parts_z)]
     for peer in peers:
         pl.semaphore_signal(barrier, inc=1, device_id=peer, device_id_type=MESH)
 
@@ -152,6 +167,8 @@
             ].astype(F32)
         if which == 0:
             pl.semaphore_wait(barrier, len(peers))
+            for peer in beyond:
+                pl.semaphore_signal(known.at[0], inc=1, device_id=peer, device_id_type=MESH)
         for turn in (0, 1):
             halo_start(which, LEVELS - 1, turn ^ core)
     for which in (0, 1):
@@ -338,9 +355,15 @@
         for which in (0, 1):
             inside(which, level)
             sides(which, level)
+            if level == LEVELS - 1 and which == 0:
+                pl.semaphore_wait(known.at[0], len(beyond))
+                for peer in farther:
+                    pl.semaphore_signal(known.at[1], inc=1, device_id=peer, device_id_type=MESH)
     inside(0, 1)
     inside(1, 1)
     sides(0, 1)
+    if farther:
+        pl.semaphore_wait(known.at[1], len(farther))
     finish(1)
     finish(0)
     for chunk, side in ((2, 1 - core), (3, core)):
@@ -478,6 +501,7 @@
             pltpu.VMEM((3, block, span), F32),
             pltpu.VMEM((3, most, block, span), F32),
             dma((5,)),
+            pltpu.SemaphoreType.REGULAR((2,)),
             dma((2, LEVELS, 2)),
             dma((2, LEVELS, 2)),
             dma((chunks, most)),

time: 66.6 us -> 66.2 us (level)
  no operation moved by 1% of the time
where the time goes in v5:
time: 66.2 us; the launch traced here: 66 us
  Pallas kernels  64.6 us (98%)
  local copies, waits for them, and re-layouts  1.31 us (2%)
    pallas_call x1, Pallas kernels, per_device(): pl.pallas_call(functools.partial(kernel, doms, float(depth * doms * width...  64.6 us

profile of v5, /device:TPU:1, one launch (start us, length us, event | category | flops | bytes accessed | tf_op | source)
XLA Modules:
  0.0 66.0 jit_solution(2783237088873838912)
XLA Ops:
  0.0 0.0 copy-start.3
  0.0 0.0 copy-start
  0.0 0.0 copy-start.1
  0.0 0.0 copy-start.2
  0.0 0.6 copy-done.3
  0.7 0.0 copy-done
  0.7 0.0 copy-done.1
  0.7 0.0 copy-done.2
  0.7 64.6 %shard_map.73 = f32[32,128]{1,0:T(8,128)S(1)} custom-call(f32[16,128,128]{2,1,0:T(8,128)} %kappa_hbm.1, bf16[2,16,128,128]{3,2,1,0:T(8,128)(2,1)} %bitcast.12, bf16[2,16,128,128]{3,2,1,0:T(8,128)(2,1)} %bitcast.13, f32[4]{0:T(128)S(1)} %bitcast.10, f32[4,256]{1,0:T(4,128)S(1)} %bitcast.8, s32[3]{0:T(128)S(1)} %bitcast.11, s32[3,1,256]{2,1,0:T(1,128)S(1)} %bitcast.9), custom_call_target="tpu_custom_call" | custom-call | tf_op jit(solution)/shard_map/pallas_call | solution.py:467
  65.4 0.6 copy.9
Async XLA Ops:
  0.0 0.7 copy-start.3
  0.0 0.7 %copy-start = (f32[1,4,256]{2,1,0:T(4,128)S(1)}, f32[1,4,256]{2,1,0:T(4,128)}, u32[]{:S(2)}) copy-start(f32[1,4,256]{2,1,0:T(4,128)} %param.11) | copy-start | bytes 12292
  0.0 0.7 %copy-start.1 = (s32[1,3,256]{2,0,1:T(1,128)S(1)}, s32[1,3,256]{2,0,1:T(1,128)}, u32[]{:S(2)}) copy-start(s32[1,3,256]{2,0,1:T(1,128)} %param.13) | copy-start | bytes 9220
  0.0 0.7 %copy-start.2 = (f32[1,4]{1,0:T(1,128)S(1)}, f32[1,4]{1,0:T(1,128)}, u32[]{:S(2)}) copy-start(f32[1,4]{1,0:T(1,128)} %param.10) | copy-start | bytes 52

commit v6 on v5

--- a/solution.py
+++ b/solution.py
@@ -53,8 +53,8 @@
 
 def kernel(
     doms, cells,
-    kappa_hbm, source_hbm, adjoint_hbm, wave, residual, cell, receiver, out,
-    kappa, given, fields, totals, part, spot, marks, row_side, column_side, inject_side,
+    kappa_hbm, source_hbm, adjoint_hbm, wave_hbm, residual_hbm, cell_hbm, receiver_hbm, out,
+    wave, residual, cell, receiver, kappa, given, fields, totals, part, spot, marks, row_side, column_side, inject_side,
     blur_row, blur_column, order,
     first_in, second_out, second_in, y_out, y_in, y_sum, power_out, power_in,
     load_sem, known, halo_send, halo_recv,
@@ -79,8 +79,8 @@
     def by_y(step):
         return (((y_at + step) % parts_y * parts_x + x_at) * parts_z + z_at, dom)
 
-    def by_dom(step):
-        return (shot, (dom + step) % doms)
+    def by_x_and_dom(step):
+        return (by_x(step // doms)[0], (dom + step) % doms)
 
     def by_ring(step, turn):
         at = (y_at * (doms // 2) + dom // 2 + step) % ring
@@ -98,6 +98,10 @@
         (
             (source_hbm.at[0], given[0][0]),
             (adjoint_hbm.at[0], given[1][0]),
+            (receiver_hbm, receiver),
+            (residual_hbm, residual),
+            (wave_hbm, wave),
+            (cell_hbm, cell),
             (kappa_hbm, kappa),
             (source_hbm.at[1], given[0][1]),
             (adjoint_hbm.at[1], given[1][1]),
@@ -109,9 +113,8 @@
 
     barrier = pltpu.get_barrier_semaphore()
     stages = (
-        [by_dom(step) for step in range(1, doms)],
         [by_z(step) for step in range(1, parts_z)],
-        [by_x(step) for step in range(1, parts_x)],
+        [by_x_and_dom(step) for step in range(1, parts_x * doms)],
     )
     beyond = [by_ring(step, 0) for step in near(ring)]
     beyond += [by_z(step) for step in near(parts_z)] + [by_x(step) for step in near(parts_x)]
@@ -176,6 +179,8 @@
             HALO : depth - HALO
         ].astype(F32)
 
+    for load in loads[2:6]:
+        load.wait()
     row_side[...] = twice(band(width, (0.0,) + RING), 1)
     column_side[...] = twice(band(span, (0.0,) + RING), 0)
     first = lax.broadcasted_iota(jnp.int32, (width, span), 0) == cell[1]
@@ -299,8 +304,8 @@
         return remote(
             part.at[pl.ds(starts[chunk], HALO), pl.ds(pl.multiple_of(place, stripe), stripe)],
             first_in[way].at[max(chunk - 1, 0), step - 1],
-            first_send.at[chunk, step - 1],
-            first_recv.at[chunk, step - 1],
+            first_send.at[chunk],
+            first_recv.at[chunk],
             (by_x, by_z)[way](step),
         )
 
@@ -309,10 +314,21 @@
         return remote(
             second_out[way].at[max(chunk - 1, 0), (spots[1 - way] + step) % first_two[way][1]],
             second_in[way].at[max(chunk - 1, 0), step - 1],
-            second_send.at[chunk, step - 1],
-            second_recv.at[chunk, step - 1],
+            second_send.at[chunk],
+            second_recv.at[chunk],
             (by_z, by_x)[way](step),
         )
+
+    def together(into, send_sem, recv_sem):
+        return remote(into, into, send_sem, recv_sem, by_x(1))
+
+    def first_all(chunk):
+        into = first_in[ways[chunk]].at[max(chunk - 1, 0)]
+        return together(into, first_send.at[chunk], first_recv.at[chunk])
+
+    def second_all(chunk):
+        into = second_in[ways[chunk]].at[max(chunk - 1, 0)]
+        return together(into, second_send.at[chunk], second_recv.at[chunk])
 
     def y_copy(chunk, step):
         return remote(
@@ -349,7 +365,7 @@
             if level > 1 or which == 0:
                 halo_start(which, level - 1, side)
 
-    for load in loads[2:]:
+    for load in loads[6:]:
         load.wait()
     for level in reversed(range(2, LEVELS)):
         for which in (0, 1):
@@ -372,25 +388,35 @@
         halo_wait(0, 0, side)
         finish(chunk)
 
-    for chunk in (1, 2, 0, 3):
+    for level in reversed(range(LEVELS)):
+        for which in (0, 1) if level > 0 else (0,):
+            for side in (0, 1):
+
+                @pl.when(beside(side)[1])
+                def _():
+                    halo_copy(which, level, side, 1 - side).wait_send()
+
+    for chunk in (1, 2, 3, 0):
         way = ways[chunk]
         parts = first_two[way]
         stripe = width // parts[0]
         own = pl.multiple_of(spots[way] * stripe, stripe)
         summed = part[pl.ds(starts[chunk], HALO), pl.ds(own, stripe)]
+        first_all(chunk).wait_recv()
         for step in first_steps(chunk):
-            first_copy(chunk, step).wait_recv()
             summed = summed + first_in[way][max(chunk - 1, 0), step - 1]
         moved = dot(order[way][...], rows_of(split(summed.reshape(HALO * stripe, span))))
         second_out[way][max(chunk - 1, 0)] = moved.reshape(parts[1], HALO * stripe // parts[1], span)
         for step in second_steps(chunk):
             second_copy(chunk, step).start()
+    for chunk in range(len(starts)):
+        first_all(chunk).wait_send()
     block = rows * HALO
     for chunk in (1, 2, 0, 3):
         way = ways[chunk]
         summed = second_out[way][max(chunk - 1, 0), spots[1 - way]]
+        second_all(chunk).wait_recv()
         for step in second_steps(chunk):
-            second_copy(chunk, step).wait_recv()
             summed = summed + second_in[way][max(chunk - 1, 0), step - 1]
         y_out[chunk] = summed.reshape(parts_y, block, span)
         for step in range(1, parts_y):
@@ -404,25 +430,28 @@
         y_sum[chunk] = summed
         for y_hi in range(parts_y):
             power = power + summed[y_hi] * summed[y_hi]
-    power_copies = []
     for stage, peers in enumerate(stages):
         power_out[stage] = power
-        now = [
+        for step, peer in enumerate(peers):
             remote(
                 power_out.at[stage],
                 power_in.at[stage, step],
-                p_send.at[stage, step],
-                p_recv.at[stage, step],
+                p_send.at[stage],
+                p_recv.at[stage],
                 peer,
-            )
-            for step, peer in enumerate(peers)
-        ]
-        for copy in now:
-            copy.start()
-        for step, copy in enumerate(now):
-            copy.wait_recv()
+            ).start()
+        if stage == 0:
+            for chunk in range(len(starts)):
+                second_all(chunk).wait_send()
+                for step in range(1, parts_y):
+                    y_copy(chunk, step).wait_send()
+        else:
+            into = power_in.at[0, pl.ds(0, len(stages[0]))]
+            together(into, p_send.at[0], p_recv.at[0]).wait_send()
+        into = power_in.at[stage, pl.ds(0, len(peers))]
+        together(into, p_send.at[stage], p_recv.at[stage]).wait_recv()
+        for step in range(len(peers)):
             power = power + power_in[stage, step]
-        power_copies += now
     scale = lax.rsqrt(jnp.full((1, 1), jnp.sum(power)) * (1.0 / cells) + 1e-6)
     for chunk, start in enumerate(starts):
         place = start * rows
@@ -430,22 +459,8 @@
             place = pl.multiple_of(place, block)
         out[pl.ds(place, block)] = -y_sum[chunk, y_at] * scale
 
-    for chunk in range(len(starts)):
-        for step in first_steps(chunk):
-            first_copy(chunk, step).wait_send()
-        for step in second_steps(chunk):
-            second_copy(chunk, step).wait_send()
-        for step in range(1, parts_y):
-            y_copy(chunk, step).wait_send()
-    for copy in power_copies:
-        copy.wait_send()
-    for level in reversed(range(LEVELS)):
-        for which in (0, 1) if level > 0 else (0,):
-            for side in (0, 1):
-
-                @pl.when(beside(side)[1])
-                def _():
-                    halo_copy(which, level, side, 1 - side).wait_send()
+    into = power_in.at[1, pl.ds(0, len(stages[1]))]
+    together(into, p_send.at[1], p_recv.at[1]).wait_send()
 
 
 def per_device(doms, kappa, source_pair, adjoint_pair, wavelet, residuals, source_cell, receiver_cells):
@@ -456,10 +471,9 @@
     chunks = depth // HALO
     counts = (HALO * width // parts_x, HALO * width // parts_z)
     block = rows * HALO
-    most = max(doms, parts_z, parts_x) - 1
-    hbm = pl.BlockSpec(memory_space=pl.ANY)
+    most = max(doms * parts_x, parts_z) - 1
+    hbm = pl.BlockSpec(memory_space=pltpu.HBM)
     vmem = pl.BlockSpec(memory_space=pltpu.VMEM)
-    smem = pl.BlockSpec(memory_space=pltpu.SMEM)
     dma = pltpu.SemaphoreType.DMA
     slab = pltpu.VMEM(kappa.shape, F32)
     padded = pltpu.VMEM((depth + 2 * HALO, width, span), F32)
@@ -467,9 +481,13 @@
     direction = pl.pallas_call(
         functools.partial(kernel, doms, float(depth * doms * width * span)),
         out_shape=jax.ShapeDtypeStruct((depth * rows, span), F32),
-        in_specs=[hbm, hbm, hbm, smem, vmem, smem, vmem],
+        in_specs=[hbm] * 7,
         out_specs=vmem,
         scratch_shapes=[
+            pltpu.SMEM(wavelet.shape[1:], F32),
+            pltpu.VMEM(residuals.shape[1:], F32),
+            pltpu.SMEM(source_cell.shape[1:], jnp.int32),
+            pltpu.VMEM((3, 1, receivers), jnp.int32),
             slab,
             [[first] * 2] * 2,
             [[padded] * LEVELS] * 2,
@@ -498,20 +516,20 @@
             pltpu.VMEM((chunks, parts_y, block, span), F32),
             pltpu.VMEM((chunks, parts_y - 1, parts_y, block, span), F32),
             pltpu.VMEM((chunks, parts_y, block, span), F32),
-            pltpu.VMEM((3, block, span), F32),
-            pltpu.VMEM((3, most, block, span), F32),
-            dma((5,)),
+            pltpu.VMEM((2, block, span), F32),
+            pltpu.VMEM((2, most, block, span), F32),
+            dma((9,)),
             pltpu.SemaphoreType.REGULAR((2,)),
             dma((2, LEVELS, 2)),
             dma((2, LEVELS, 2)),
-            dma((chunks, most)),
-            dma((chunks, most)),
-            dma((chunks, most)),
-            dma((chunks, most)),
+            dma((chunks,)),
+            dma((chunks,)),
+            dma((chunks,)),
+            dma((chunks,)),
             dma((chunks, parts_y - 1)),
             dma((chunks, parts_y - 1)),
-            dma((3, most)),
-            dma((3, most)),
+            dma((2,)),
+            dma((2,)),
         ],
         compiler_params=pltpu.CompilerParams(
             collective_id=0, has_side_effects=True, vmem_limit_bytes=56164352

time: 66.2 us -> 64.5 us (0.974)
  Pallas kernels: 64.6 us -> 63 us
    pallas_call x1, Pallas kernels: 64.6 us -> 63 us  [per_device(): pl.pallas_call(functools.partial(kernel, doms, float(depth * doms * width...]
where the time goes in v6:
time: 64.5 us; the launch traced here: 64.3 us
  Pallas kernels  63 us (98%)
  local copies, waits for them, and re-layouts  1.31 us (2%)
    pallas_call x1, Pallas kernels, per_device(): pl.pallas_call(functools.partial(kernel, doms, float(depth * doms * width...  63 us
    unnamed x9, local copies, waits for them, and re-layouts  1.31 us

profile of v6, /device:TPU:1, one launch (start us, length us, event | category | flops | bytes accessed | tf_op | source)
XLA Modules:
  0.0 64.3 jit_solution(6777860239851122301)
XLA Ops:
  0.0 0.0 copy-start.3
  0.0 0.0 copy-start
  0.0 0.0 copy-start.1
  0.0 0.0 copy-start.2
  0.0 0.6 copy-done.3
  0.7 0.0 copy-done
  0.7 0.0 copy-done.1
  0.7 0.0 copy-done.2
  0.7 63.0 %shard_map.73 = f32[32,128]{1,0:T(8,128)S(1)} custom-call(f32[16,128,128]{2,1,0:T(8,128)} %kappa_hbm.1, bf16[2,16,128,128]{3,2,1,0:T(8,128)(2,1)} %bitcast.12, bf16[2,16,128,128]{3,2,1,0:T(8,128)(2,1)} %bitcast.13, f32[4]{0:T(128)S(1)} %bitcast.10, f32[4,256]{1,0:T(4,128)S(1)} %bitcast.8, s32[3]{0:T(128)S(1)} %bitcast.11, s32[3,1,256]{2,1,0:T(1,128)S(1)} %bitcast.9), custom_call_target="tpu_custom_call" | custom-call | tf_op jit(solution)/shard_map/pallas_call | solution.py:481
  63.7 0.6 copy.9
Async XLA Ops:
  0.0 0.7 %copy-start.3 = (s32[1,3]{1,0:T(1,128)S(1)}, s32[1,3]{1,0:T(1,128)}, u32[]{:S(2)}) copy-start(s32[1,3]{1,0:T(1,128)} %param.12) | copy-start | bytes 40
  0.0 0.7 %copy-start = (f32[1,4,256]{2,1,0:T(4,128)S(1)}, f32[1,4,256]{2,1,0:T(4,128)}, u32[]{:S(2)}) copy-start(f32[1,4,256]{2,1,0:T(4,128)} %param.11) | copy-start | bytes 12292
  0.0 0.7 %copy-start.1 = (s32[1,3,256]{2,0,1:T(1,128)S(1)}, s32[1,3,256]{2,0,1:T(1,128)}, u32[]{:S(2)}) copy-start(s32[1,3,256]{2,0,1:T(1,128)} %param.13) | copy-start | bytes 9220
  0.0 0.7 %copy-start.2 = (f32[1,4]{1,0:T(1,128)S(1)}, f32[1,4]{1,0:T(1,128)}, u32[]{:S(2)}) copy-start(f32[1,4]{1,0:T(1,128)} %param.10) | copy-start | bytes 52

commit v7 on v6

--- a/solution.py
+++ b/solution.py
@@ -124,18 +124,6 @@
     for peer in peers:
         pl.semaphore_signal(barrier, inc=1, device_id=peer, device_id_type=MESH)
 
-    @pl.when(dom == 0)
-    def _():
-        for which in (0, 1):
-            for level in range(LEVELS):
-                fields[which][level][0:HALO] = jnp.zeros((HALO, width, span), F32)
-
-    @pl.when(dom == doms - 1)
-    def _():
-        for which in (0, 1):
-            for level in range(LEVELS):
-                fields[which][level][HALO + depth :] = jnp.zeros((HALO, width, span), F32)
-
     def beside(side):
         neighbour = dom + 2 * side - 1
         return neighbour, (neighbour >= 0) & (neighbour < doms)
@@ -174,6 +162,18 @@
                 pl.semaphore_signal(known.at[0], inc=1, device_id=peer, device_id_type=MESH)
         for turn in (0, 1):
             halo_start(which, LEVELS - 1, turn ^ core)
+    @pl.when(dom == 0)
+    def _():
+        for which in (0, 1):
+            for level in range(LEVELS):
+                fields[which][level][0:HALO] = jnp.zeros((HALO, width, span), F32)
+
+    @pl.when(dom == doms - 1)
+    def _():
+        for which in (0, 1):
+            for level in range(LEVELS):
+                fields[which][level][HALO + depth :] = jnp.zeros((HALO, width, span), F32)
+
     for which in (0, 1):
         fields[which][LEVELS - 1][2 * HALO : depth] = given[which][0][
             HALO : depth - HALO
@@ -376,11 +376,12 @@
                 for peer in farther:
                     pl.semaphore_signal(known.at[1], inc=1, device_id=peer, device_id_type=MESH)
     inside(0, 1)
-    inside(1, 1)
+    advance(1, 1, starts[1])
     sides(0, 1)
     if farther:
         pl.semaphore_wait(known.at[1], len(farther))
     finish(1)
+    advance(1, 1, starts[0])
     finish(0)
     for chunk, side in ((2, 1 - core), (3, core)):
         halo_wait(1, 1, side)
@@ -430,6 +431,7 @@
         y_sum[chunk] = summed
         for y_hi in range(parts_y):
             power = power + summed[y_hi] * summed[y_hi]
+    power = jnp.sum(power, axis=0, keepdims=True)
     for stage, peers in enumerate(stages):
         power_out[stage] = power
         for step, peer in enumerate(peers):
@@ -516,8 +518,8 @@
             pltpu.VMEM((chunks, parts_y, block, span), F32),
             pltpu.VMEM((chunks, parts_y - 1, parts_y, block, span), F32),
             pltpu.VMEM((chunks, parts_y, block, span), F32),
-            pltpu.VMEM((2, block, span), F32),
-            pltpu.VMEM((2, most, block, span), F32),
+            pltpu.VMEM((2, 1, span), F32),
+            pltpu.VMEM((2, most, 1, span), F32),
             dma((9,)),
             pltpu.SemaphoreType.REGULAR((2,)),
             dma((2, LEVELS, 2)),

time: 64.5 us -> 63.5 us (0.984)
  Pallas kernels: 63 us -> 62 us
    pallas_call x1, Pallas kernels: 63 us -> 62 us  [per_device(): pl.pallas_call(functools.partial(kernel, doms, float(depth * doms * width...]
where the time goes in v7:
time: 63.5 us; the launch traced here: 63.4 us
  Pallas kernels  62 us (98%)
  local copies, waits for them, and re-layouts  1.31 us (2%)
    pallas_call x1, Pallas kernels, per_device(): pl.pallas_call(functools.partial(kernel, doms, float(depth * doms * width...  62 us
    unnamed x9, local copies, waits for them, and re-layouts  1.31 us

profile of v7, /device:TPU:1, one launch (start us, length us, event | category | flops | bytes accessed | tf_op | source)
XLA Modules:
  0.0 63.4 jit_solution(14573591318367498820)
XLA Ops:
  0.0 0.0 copy-start.3
  0.0 0.0 copy-start
  0.0 0.0 copy-start.1
  0.0 0.0 copy-start.2
  0.0 0.6 %copy-done.3 = s32[1,3]{1,0:T(1,128)S(1)} copy-done((s32[1,3]{1,0:T(1,128)S(1)}, s32[1,3]{1,0:T(1,128)}, u32[]{:S(2)}) %copy-start.3) | copy-done | bytes 36
  0.7 0.0 copy-done
  0.7 0.0 copy-done.1
  0.7 0.0 copy-done.2
  0.7 62.0 %shard_map.73 = f32[32,128]{1,0:T(8,128)S(1)} custom-call(f32[16,128,128]{2,1,0:T(8,128)} %kappa_hbm.1, bf16[2,16,128,128]{3,2,1,0:T(8,128)(2,1)} %bitcast.12, bf16[2,16,128,128]{3,2,1,0:T(8,128)(2,1)} %bitcast.13, f32[4]{0:T(128)S(1)} %bitcast.10, f32[4,256]{1,0:T(4,128)S(1)} %bitcast.8, s32[3]{0:T(128)S(1)} %bitcast.11, s32[3,1,256]{2,1,0:T(1,128)S(1)} %bitcast.9), custom_call_target="tpu_custom_call" | custom-call | tf_op jit(solution)/shard_map/pallas_call | solution.py:483
  62.8 0.6 copy.9
Async XLA Ops:
  0.0 0.7 %copy-start.3 = (s32[1,3]{1,0:T(1,128)S(1)}, s32[1,3]{1,0:T(1,128)}, u32[]{:S(2)}) copy-start(s32[1,3]{1,0:T(1,128)} %param.12) | copy-start | bytes 40
  0.0 0.7 %copy-start = (f32[1,4,256]{2,1,0:T(4,128)S(1)}, f32[1,4,256]{2,1,0:T(4,128)}, u32[]{:S(2)}) copy-start(f32[1,4,256]{2,1,0:T(4,128)} %param.11) | copy-start | bytes 12292
  0.0 0.7 %copy-start.1 = (s32[1,3,256]{2,0,1:T(1,128)S(1)}, s32[1,3,256]{2,0,1:T(1,128)}, u32[]{:S(2)}) copy-start(s32[1,3,256]{2,0,1:T(1,128)} %param.13) | copy-start | bytes 9220
  0.0 0.7 %copy-start.2 = (f32[1,4]{1,0:T(1,128)S(1)}, f32[1,4]{1,0:T(1,128)}, u32[]{:S(2)}) copy-start(f32[1,4]{1,0:T(1,128)} %param.10) | copy-start | bytes 52

commit v8 on v7

--- a/solution.py
+++ b/solution.py
@@ -10,9 +10,9 @@
 MESH = pl.DeviceIdType.MESH
 LEVELS = 4
 HALO = 4
-SCALE = 5040.0
-RING = (8064.0, -1008.0, 128.0, -9.0)
-CENTER = 3.0 * -14350.0
+SCALE = 5040.0 / 128.0
+RING = (63.0, -7.875, 1.0, -0.0703125)
+CENTER = (-336.0, -0.328125)
 SHOT_PARTS = (2, 4, 8)
 F32 = jnp.float32
 BF16 = jnp.bfloat16
@@ -181,8 +181,8 @@
 
     for load in loads[2:6]:
         load.wait()
-    row_side[...] = twice(band(width, (0.0,) + RING), 1)
-    column_side[...] = twice(band(span, (0.0,) + RING), 0)
+    row_side[...] = twice(band(width, CENTER[1:] + RING), 1)
+    column_side[...] = twice(band(span, CENTER[:1] + RING), 0)
     first = lax.broadcasted_iota(jnp.int32, (width, span), 0) == cell[1]
     second = lax.broadcasted_iota(jnp.int32, (width, span), 1) == cell[2]
     spot[...] = jnp.where(first & second, 1.0, 0.0)
@@ -253,12 +253,13 @@
         for at in layers:
             z = start + at
             current = field[z + HALO]
-            summed = lateral[at] + CENTER * current
+            summed = lateral[at]
             for shift in range(1, HALO + 1):
-                summed = summed + RING[shift - 1] * (
-                    field[z + HALO + shift] + field[z + HALO - shift]
-                )
-            term = kappa[z] * (summed * (1.0 / SCALE)) + inject[at]
+                pair = field[z + HALO + shift] + field[z + HALO - shift]
+                if RING[shift - 1] != 1.0:
+                    pair = RING[shift - 1] * pair
+                summed = summed + pair
+            term = kappa[z] * summed + inject[at]
             if which == 0:
                 product = fields[1][level][z + HALO] * term
                 if level < LEVELS - 1:
@@ -367,6 +368,7 @@
 
     for load in loads[6:]:
         load.wait()
+    kappa[...] = kappa[...] * (1.0 / SCALE)
     for level in reversed(range(2, LEVELS)):
         for which in (0, 1):
             inside(which, level)

time: 63.5 us -> 63.3 us (level)
  no operation moved by 1% of the time
where the time goes in v8:
time: 63.3 us; the launch traced here: 63.1 us
  Pallas kernels  61.8 us (98%)
  local copies, waits for them, and re-layouts  1.31 us (2%)
    pallas_call x1, Pallas kernels, per_device(): pl.pallas_call(functools.partial(kernel, doms, float(depth * doms * width...  61.8 us
    unnamed x9, local copies, waits for them, and re-layouts  1.31 us

profile of v8, /device:TPU:1, one launch (start us, length us, event | category | flops | bytes accessed | tf_op | source)
XLA Modules:
  0.0 63.1 jit_solution(4646782656205262228)
XLA Ops:
  0.0 0.0 copy-start.3
  0.0 0.0 copy-start
  0.0 0.0 copy-start.1
  0.0 0.0 copy-start.2
  0.0 0.6 %copy-done.3 = s32[1,3]{1,0:T(1,128)S(1)} copy-done((s32[1,3]{1,0:T(1,128)S(1)}, s32[1,3]{1,0:T(1,128)}, u32[]{:S(2)}) %copy-start.3) | copy-done | bytes 36
  0.7 0.0 copy-done
  0.7 0.0 copy-done.1
  0.7 0.0 copy-done.2
  0.7 61.8 %shard_map.73 = f32[32,128]{1,0:T(8,128)S(1)} custom-call(f32[16,128,128]{2,1,0:T(8,128)} %kappa_hbm.1, bf16[2,16,128,128]{3,2,1,0:T(8,128)(2,1)} %bitcast.12, bf16[2,16,128,128]{3,2,1,0:T(8,128)(2,1)} %bitcast.13, f32[4]{0:T(128)S(1)} %bitcast.10, f32[4,256]{1,0:T(4,128)S(1)} %bitcast.8, s32[3]{0:T(128)S(1)} %bitcast.11, s32[3,1,256]{2,1,0:T(1,128)S(1)} %bitcast.9), custom_call_target="tpu_custom_call" | custom-call | tf_op jit(solution)/shard_map/pallas_call | solution.py:485
  62.5 0.6 copy.9
Async XLA Ops:
  0.0 0.7 %copy-start.3 = (s32[1,3]{1,0:T(1,128)S(1)}, s32[1,3]{1,0:T(1,128)}, u32[]{:S(2)}) copy-start(s32[1,3]{1,0:T(1,128)} %param.12) | copy-start | bytes 40
  0.0 0.7 %copy-start = (f32[1,4,256]{2,1,0:T(4,128)S(1)}, f32[1,4,256]{2,1,0:T(4,128)}, u32[]{:S(2)}) copy-start(f32[1,4,256]{2,1,0:T(4,128)} %param.11) | copy-start | bytes 12292
  0.0 0.7 %copy-start.1 = (s32[1,3,256]{2,0,1:T(1,128)S(1)}, s32[1,3,256]{2,0,1:T(1,128)}, u32[]{:S(2)}) copy-start(s32[1,3,256]{2,0,1:T(1,128)} %param.13) | copy-start | bytes 9220
  0.0 0.7 %copy-start.2 = (f32[1,4]{1,0:T(1,128)S(1)}, f32[1,4]{1,0:T(1,128)}, u32[]{:S(2)}) copy-start(f32[1,4]{1,0:T(1,128)} %param.10) | copy-start | bytes 52

commit v9 on v7

--- a/solution.py
+++ b/solution.py
@@ -37,6 +37,10 @@
 def twice(matrix, axis):
     matrix = matrix.astype(BF16)
     return jnp.concatenate((matrix, matrix), axis=axis)
+
+
+def far_first(size):
+    return sorted(range(1, size), key=lambda step: -min(step, size - step))
 
 
 def dot(a, b):
@@ -113,8 +117,13 @@
 
     barrier = pltpu.get_barrier_semaphore()
     stages = (
-        [by_z(step) for step in range(1, parts_z)],
-        [by_x_and_dom(step) for step in range(1, parts_x * doms)],
+        [by_z(step) for step in far_first(parts_z)],
+        [
+            by_x_and_dom(step * doms + at)
+            for step in far_first(parts_x) + [0]
+            for at in range(doms)
+            if step or at
+        ],
     )
     beyond = [by_ring(step, 0) for step in near(ring)]
     beyond += [by_z(step) for step in near(parts_z)] + [by_x(step) for step in near(parts_x)]
@@ -340,10 +349,10 @@
         )
 
     def first_steps(chunk):
-        return range(1, first_two[ways[chunk]][0])
+        return far_first(first_two[ways[chunk]][0])
 
     def second_steps(chunk):
-        return range(1, first_two[ways[chunk]][1])
+        return far_first(first_two[ways[chunk]][1])
 
     def finish(chunk):
         start = starts[chunk]

time: 63.5 us -> 63 us (level)
  no operation moved by 1% of the time
where the time goes in v9:
time: 63 us; the launch traced here: 62.9 us
  Pallas kernels  61.5 us (98%)
  local copies, waits for them, and re-layouts  1.31 us (2%)
    pallas_call x1, Pallas kernels, per_device(): pl.pallas_call(functools.partial(kernel, doms, float(depth * doms * width...  61.5 us
    unnamed x9, local copies, waits for them, and re-layouts  1.31 us

profile of v9, /device:TPU:1, one launch (start us, length us, event | category | flops | bytes accessed | tf_op | source)
XLA Modules:
  0.0 62.9 jit_solution(15103477057847393565)
XLA Ops:
  0.0 0.0 copy-start.3
  0.0 0.0 copy-start
  0.0 0.0 copy-start.1
  0.0 0.0 copy-start.2
  0.0 0.6 %copy-done.3 = s32[1,3]{1,0:T(1,128)S(1)} copy-done((s32[1,3]{1,0:T(1,128)S(1)}, s32[1,3]{1,0:T(1,128)}, u32[]{:S(2)}) %copy-start.3) | copy-done | bytes 36
  0.7 0.0 copy-done
  0.7 0.0 copy-done.1
  0.7 0.0 copy-done.2
  0.7 61.5 %shard_map.73 = f32[32,128]{1,0:T(8,128)S(1)} custom-call(f32[16,128,128]{2,1,0:T(8,128)} %kappa_hbm.1, bf16[2,16,128,128]{3,2,1,0:T(8,128)(2,1)} %bitcast.12, bf16[2,16,128,128]{3,2,1,0:T(8,128)(2,1)} %bitcast.13, f32[4]{0:T(128)S(1)} %bitcast.10, f32[4,256]{1,0:T(4,128)S(1)} %bitcast.8, s32[3]{0:T(128)S(1)} %bitcast.11, s32[3,1,256]{2,1,0:T(1,128)S(1)} %bitcast.9), custom_call_target="tpu_custom_call" | custom-call | tf_op jit(solution)/shard_map/pallas_call | solution.py:492
  62.3 0.6 copy.9
Async XLA Ops:
  0.0 0.7 %copy-start.3 = (s32[1,3]{1,0:T(1,128)S(1)}, s32[1,3]{1,0:T(1,128)}, u32[]{:S(2)}) copy-start(s32[1,3]{1,0:T(1,128)} %param.12) | copy-start | bytes 40
  0.0 0.7 %copy-start = (f32[1,4,256]{2,1,0:T(4,128)S(1)}, f32[1,4,256]{2,1,0:T(4,128)}, u32[]{:S(2)}) copy-start(f32[1,4,256]{2,1,0:T(4,128)} %param.11) | copy-start | bytes 12292
  0.0 0.7 %copy-start.1 = (s32[1,3,256]{2,0,1:T(1,128)S(1)}, s32[1,3,256]{2,0,1:T(1,128)}, u32[]{:S(2)}) copy-start(s32[1,3,256]{2,0,1:T(1,128)} %param.13) | copy-start | bytes 9220
  0.0 0.7 %copy-start.2 = (f32[1,4]{1,0:T(1,128)S(1)}, f32[1,4]{1,0:T(1,128)}, u32[]{:S(2)}) copy-start(f32[1,4]{1,0:T(1,128)} %param.10) | copy-start | bytes 52
